TPU v7x, 512 devices: a whole 4x4x16 slice. The times are simulated.
512 devices in a mesh: seq: 64 (over z, y_lo, core), head: 8 (over y_hi, x).
Axes of the slice: x: 4, y: 4 (y_hi: 2, y_lo: 2; y = y_hi * 2 + y_lo), z: 16, core: 2. Of those that a mesh axis runs over, the one named last changes fastest.
Arguments:
- queries: bfloat16 [64, 64, 1, 3072], P('seq', 'head'), may hold values from -150 to 150
- keys: bfloat16 [64, 64, 1, 3072], P('seq', 'head'), may hold values from -6.1 to 6.1
- values: bfloat16 [64, 64, 1, 3072], P('seq', 'head'), may hold values from -6 to 6
- text_keys: bfloat16 [256, 3072], P(None, 'head'), may hold values from -6 to 6
- text_values: bfloat16 [256, 3072], P(None, 'head'), may hold values from -6 to 6
- text_mask: int32 [256], replicated, may hold values from 0 to 1, as said below
- tokens: bfloat16 [64, 64, 1, 3072], P('seq', 'head'), may hold values from -6 to 6
- out_weight: bfloat16 [3072, 3072], P('head'), may hold values from -0.109375 to 0.109375
- out_bias: float32 [3072], replicated, may hold values from -3 to 3
- gate: float32 [3072], replicated, may hold values from -4 to 4
- shift: float32 [3072], replicated, may hold values from -4 to 4
- scale: float32 [3072], replicated, may hold values from -2.5 to 2.5
- final_weight: bfloat16 [3072, 64], replicated, may hold values from -0.109375 to 0.109375
- final_bias: float32 [64], replicated, may hold values from -3 to 3
- conv_weight: bfloat16 [3, 3, 3, 16, 512], replicated, may hold values from -0.3125 to 0.3125
- conv_bias: float32 [512], replicated, may hold values from -3 to 3
Outputs:
- block_out: bfloat16 [64, 64, 1, 3072], P('seq', 'head')
- decoded: bfloat16 [1, 128, 128, 512], P(None, 'seq', 'head')
Inputs may be any that keep to these rules, and one draw needn't show every extreme that they name: text_mask is 1 on a leading run of real text tokens and 0 on the padding after it; the first entry is always 1 and the last always 0.
All inputs are finite; a program needn't handle non-finite values.
Results may differ from a plain program's by a relative error of at most 0.017.
Values may be sent and summed in bfloat16 or wider, within the bound.
A program may use at most 64 MiB of HBM per device.

v0:
```python
import math

import jax
import jax.numpy as jnp
from jax import lax
from jax.sharding import PartitionSpec as P

D = 3072
HEAD_DIM = 128
LAT_CH = 16


NEG = -1e30
LATENT_SCALE = 0.476986


def with_halo(cells, sides, width):
    for axis, dim in sides:
        count = lax.axis_size(axis)
        ends = count - 1
        head = lax.slice_in_dim(cells, 0, width, axis=dim)
        tail = lax.slice_in_dim(cells, cells.shape[dim] - width, cells.shape[dim], axis=dim)
        cells = jnp.concatenate(
            [
                lax.ppermute(tail, axis, [(i, (i + 1) % count) for i in range(ends)]),
                cells,
                lax.ppermute(head, axis, [((i + 1) % count, i) for i in range(ends)]),
            ],
            axis=dim,
        )
    return cells


def absorb(carry, queries, block_keys, block_values, valid):
    running_max, total, accum = carry
    scores = jnp.einsum(
        "gqe,kge->gqk", queries, block_keys, preferred_element_type=jnp.float32
    ) * queries.shape[2] ** (-0.5)
    scores = jnp.where(valid[None, None, :], scores, NEG)
    new_max = jnp.maximum(running_max, jnp.max(scores, axis=2))
    factor = jnp.exp(running_max - new_max)
    weights = jnp.where(valid[None, None, :], jnp.exp(scores - new_max[:, :, None]), 0.0)
    total = total * factor + jnp.sum(weights, axis=2)
    accum = accum * factor[:, :, None] + jnp.einsum(
        "gqk,kge->gqe",
        weights.astype(jnp.bfloat16),
        block_values,
        preferred_element_type=jnp.float32,
    )
    return (new_max, total, accum)


def edge_copy(framed, first_tile, last_tile, dim):
    length = framed.shape[dim]
    outer_low = lax.slice_in_dim(framed, 0, 1, axis=dim)
    inner_low = lax.slice_in_dim(framed, 1, 2, axis=dim)
    inner_high = lax.slice_in_dim(framed, length - 2, length - 1, axis=dim)
    outer_high = lax.slice_in_dim(framed, length - 1, length, axis=dim)
    middle = lax.slice_in_dim(framed, 1, length - 1, axis=dim)
    lower_rim = jnp.where(first_tile, inner_low, outer_low)
    upper_rim = jnp.where(last_tile, inner_high, outer_high)
    return jnp.concatenate([lower_rim, middle, upper_rim], dim)


def body(
    queries,
    keys,
    values,
    text_keys,
    text_values,
    text_mask,
    tokens,
    out_weight,
    out_bias,
    gate,
    shift,
    scale,
    final_weight,
    final_bias,
    conv_weight,
    conv_bias,
):
    local_q, local_k, local_v = (
        lax.all_to_all(queries, "head", split_axis=3, concat_axis=1, tiled=True),
        lax.all_to_all(keys, "head", split_axis=3, concat_axis=1, tiled=True),
        lax.all_to_all(values, "head", split_axis=3, concat_axis=1, tiled=True),
    )
    groups = local_q.shape[3] // HEAD_DIM
    columns = local_q.shape[1]
    frames = local_q.shape[2]
    query_rows = columns * frames
    q_heads = local_q.reshape(query_rows, groups, HEAD_DIM).transpose(1, 0, 2)
    start_state = (
        jnp.full((groups, query_rows), NEG, jnp.float32),
        jnp.zeros((groups, query_rows), jnp.float32),
        jnp.zeros((groups, query_rows, HEAD_DIM), jnp.float32),
    )
    carry = absorb(
        start_state,
        q_heads,
        text_keys.reshape(-1, groups, HEAD_DIM),
        text_values.reshape(-1, groups, HEAD_DIM),
        text_mask == 1,
    )
    all_k, all_v = (
        lax.all_gather(local_k, "seq", axis=0, tiled=True),
        lax.all_gather(local_v, "seq", axis=0, tiled=True),
    )
    count = all_k.shape[0] * columns * frames
    block = math.gcd(count, 1024)
    every = jnp.ones((block,), bool)

    def step(state, pair):
        return (absorb(state, q_heads, pair[0], pair[1], every), None)

    carry, unused = lax.scan(
        step,
        carry,
        (
            all_k.reshape(count // block, block, groups, HEAD_DIM),
            all_v.reshape(count // block, block, groups, HEAD_DIM),
        ),
    )
    running_max, total, accum = carry
    attended = (accum / total[:, :, None]).astype(jnp.bfloat16)
    attended = attended.transpose(1, 0, 2).reshape(columns, frames, groups * HEAD_DIM)
    own_cols = queries.shape[1]
    partial_value = jnp.einsum(
        "cfe,ed->cfd", attended, out_weight, preferred_element_type=jnp.float32
    )
    summed = lax.psum(partial_value.astype(jnp.bfloat16), "head").astype(jnp.float32)
    projected = lax.dynamic_slice_in_dim(summed, lax.axis_index("head") * own_cols, own_cols, 0)
    stream = tokens[0].astype(jnp.float32) + gate * (projected + out_bias)
    block_out = stream.astype(jnp.bfloat16)
    normed_in = block_out.astype(jnp.float32)
    centered = normed_in - jnp.mean(normed_in, axis=2, keepdims=True)
    spread = jnp.mean(centered * centered, axis=2, keepdims=True)
    normed = centered * lax.rsqrt(spread + 1e-06)
    modulated = (normed * (1.0 + scale) + shift).astype(jnp.bfloat16)
    patches = (
        jnp.dot(modulated.reshape(-1, D), final_weight, preferred_element_type=jnp.float32)
        + final_bias
    ) / LATENT_SCALE
    latent = patches.reshape(own_cols, frames, LAT_CH, 2, 2).transpose(1, 3, 0, 4, 2)
    latent = latent.reshape(frames, 2, 2 * own_cols, LAT_CH).astype(jnp.bfloat16)
    framed = with_halo(latent, (("seq", 1), ("head", 2)), 1)
    row_place = lax.axis_index("seq")
    col_place = lax.axis_index("head")
    framed = edge_copy(framed, row_place == 0, row_place == lax.axis_size("seq") - 1, 1)
    framed = edge_copy(framed, col_place == 0, col_place == lax.axis_size("head") - 1, 2)
    timed = jnp.concatenate([framed, framed, framed], 0)
    windows = []
    for tap_t in range(3):
        for tap_i in range(3):
            for tap_j in range(3):
                windows.append(
                    timed[
                        tap_t : tap_t + frames, tap_i : tap_i + 2, tap_j : tap_j + 2 * own_cols, :
                    ]
                )
    stacked = jnp.concatenate(windows, 3).reshape(-1, 27 * LAT_CH)
    flat_weight = conv_weight.reshape(27 * LAT_CH, conv_weight.shape[4])
    decoded = jnp.dot(stacked, flat_weight, preferred_element_type=jnp.float32) + conv_bias
    decoded = decoded.reshape(frames, 2, 2 * own_cols, conv_weight.shape[4]).astype(jnp.bfloat16)
    return (block_out.reshape(1, own_cols, frames, D), decoded)


def solution(mesh):
    in_specs = (
        P("seq", "head", None, None),
        P("seq", "head", None, None),
        P("seq", "head", None, None),
        P(None, "head"),
        P(None, "head"),
        P(),
        P("seq", "head", None, None),
        P("head", None),
        P(),
        P(),
        P(),
        P(),
        P(),
        P(),
        P(),
        P(),
    )
    out_specs = (P("seq", "head", None, None), P(None, "seq", "head", None))
    return jax.shard_map(body, mesh=mesh, in_specs=in_specs, out_specs=out_specs, check_vma=False)
```

profile of v0, /device:TPU:1, one launch (start us, length us, event | category | flops | bytes accessed | tf_op | source)
XLA Modules:
  0.0 446.7 jit_solution(7458883897447124687)
XLA Ops:
  7.2 3.7 copy.74
  10.9 0.5 broadcast.68
  11.4 18.0 %reduce.3 = bf16[3072,8]{1,0:T(8,128)(2,1)S(1)} reduce(bf16[3072,1,1,8]{3,2,1,0:T(2,128)(2,1)} %bitcast.122, bf16[]{:T(256)} %broadcast.68), dimensions={1,2}, to_apply=%bitcast.90.reduce_sub_computation | reduce | bytes 98306
  29.5 0.8 reshape.172
  30.2 14.0 %all_to_all.51 = bf16[8,2,1536]{2,1,0:T(2,128)(2,1)S(1)} all-to-all(bf16[8,2,1536]{2,1,0:T(2,128)(2,1)S(1)} %reshape.172), channel_id=1, replica_groups=mesh['seq'=64,'head'=8] {'head'}, dimensions={0} | all-to-all | bytes 98304 | tf_op jit(solution)/shard_map/all_to_all | solution.py:85
  44.2 3.0 reshape.173
  47.2 3.3 copy.75
  50.5 0.6 copy.106
  51.4 2.9 copy.77
  54.3 18.0 %reduce.4 = bf16[3072,8]{1,0:T(8,128)(2,1)S(1)} reduce(bf16[3072,1,1,8]{3,2,1,0:T(2,128)(2,1)} %bitcast.127, bf16[]{:T(256)} %broadcast.68), dimensions={1,2}, to_apply=%bitcast.92.reduce_sub_computation | reduce | bytes 98306
  72.3 0.8 reshape.174
  73.1 9.0 %all_to_all.52 = bf16[8,2,1536]{2,1,0:T(2,128)(2,1)S(1)} all-to-all(bf16[8,2,1536]{2,1,0:T(2,128)(2,1)S(1)} %reshape.174), channel_id=1, replica_groups=mesh['seq'=64,'head'=8] {'head'}, dimensions={0} | all-to-all | bytes 98304 | tf_op jit(solution)/shard_map/all_to_all | solution.py:86
  82.2 3.0 reshape.175
  85.2 3.3 copy.78
  88.5 0.6 copy.105
  89.2 3.5 copy.66
  92.7 18.0 %reduce.2 = bf16[3072,8]{1,0:T(8,128)(2,1)S(1)} reduce(bf16[3072,1,1,8]{3,2,1,0:T(2,128)(2,1)} %bitcast.125, bf16[]{:T(256)} %broadcast.68), dimensions={1,2}, to_apply=%bitcast.88.reduce_sub_computation | reduce | bytes 98306
  110.7 1.4 reshape.170
  112.2 3.3 all-to-all-start
  115.9 6.2 %all-to-all-done = bf16[8,2,1536]{2,1,0:T(2,128)(2,1)S(1)} async-done(((bf16[8,2,1536]{2,1,0:T(2,128)(2,1)}), bf16[8,2,1536]{2,1,0:T(2,128)(2,1)S(1)}, u32[]{:S(2)}, u32[]{:S(2)}) %all-to-all-start) | async-done | bytes 49184 | tf_op jit(solution)/shard_map/all_to_all | solution.py:84
  122.1 3.0 reshape.171
  125.1 3.3 copy.67
  129.2 47.7 %all-gather.3.cloned.1.call-done = bf16[64,64,1,384]{3,1,2,0:T(8,128)(2,1)} async-done(((bf16[1,64,1,384]{3,1,2,0:T(8,128)(2,1)}), bf16[64,64,1,384]{3,1,2,0:T(8,128)(2,1)}) %all-gather.3.cloned.1.call-update) | async-done | bytes 3145744 | tf_op jit(solution)/shard_map/all_gather | solution.py:106
  176.9 9.0 %reshape.163 = bf16[4,1024,3,128]{3,2,1,0:T(4,128)(2,1)} reshape(bf16[64,64,1,384]{3,1,2,0:T(8,128)(2,1)} %all-gather.3.cloned.1.call-done) | data formatting | bytes 6291456 | tf_op jit(solution)/shard_map/reshape | solution.py:120
  185.9 4.5 %copy.80 = bf16[4,1024,3,128]{3,1,2,0:T(8,128)(2,1)} copy(bf16[4,1024,3,128]{3,2,1,0:T(4,128)(2,1)} %reshape.163) | data formatting | bytes 6291456 | tf_op jit(solution)/shard_map/while | solution.py:116
  190.4 108.5 %all-gather.5.cloned.1.call-done = bf16[64,64,1,384]{3,1,2,0:T(8,128)(2,1)} async-done(((bf16[1,64,1,384]{3,1,2,0:T(8,128)(2,1)}), bf16[64,64,1,384]{3,1,2,0:T(8,128)(2,1)}) %all-gather.5.cloned.1.call-update) | async-done | bytes 3145744 | tf_op jit(solution)/shard_map/all_gather | solution.py:107
  298.9 9.0 %reshape.164 = bf16[4,1024,3,128]{3,2,1,0:T(4,128)(2,1)} reshape(bf16[64,64,1,384]{3,1,2,0:T(8,128)(2,1)} %all-gather.5.cloned.1.call-done) | data formatting | bytes 6291456 | tf_op jit(solution)/shard_map/reshape | solution.py:121
  307.8 4.6 %copy.81 = bf16[4,1024,3,128]{3,1,2,0:T(8,128)(2,1)} copy(bf16[4,1024,3,128]{3,2,1,0:T(4,128)(2,1)} %reshape.164) | data formatting | bytes 6291456 | tf_op jit(solution)/shard_map/while | solution.py:116
  312.4 13.6 %while.14 = (s32[]{:T(128)}, f32[3,64]{1,0:T(4,128)S(1)}, f32[3,64]{1,0:T(4,128)S(1)}, f32[3,64,128]{2,1,0:T(8,128)S(1)}, bf16[4,1024,3,128]{3,1,2,0:T(8,128)(2,...) while((s32[]{:T(128)}, f32[3,64]{1,0:T(4,128)S(1)}, ...), condition=%wide.region_5.6_spmd, body=%wide.region_2.5_spmd.sunk | while | flops 101892480 | bytes 4191317 | solution.py:116
  312.4 1.6 fusion.66
  314.3 1.5 convolution_add_fusion.5
  315.8 1.6 fusion.66
  317.7 1.5 convolution_add_fusion.5
  319.2 1.6 fusion.66
  321.1 1.5 convolution_add_fusion.5
  322.6 1.6 fusion.66
  324.2 0.3 fusion.67
  324.5 1.5 convolution_add_fusion.5
  326.1 1.3 fusion.11
  327.5 91.0 %all-reduce.2.cloned.1.call-done = bf16[64,1,3072]{2,0,1:T(8,128)(2,1)} async-done(((bf16[64,1,3072]{2,0,1:T(8,128)(2,1)}), bf16[64,1,3072]{2,0,1:T(8,128)(2,1)}) %all-reduce.2.cloned.1.call-update) | async-done | bytes 393232 | tf_op jit(solution)/shard_map/psum | solution.py:131
  418.6 0.9 convert_reduce_fusion
  420.2 8.2 %collective-permute-start = (bf16[1,1,16,16]{3,2,1,0:T(8,128)(2,1)S(1)}, bf16[1,1,16,16]{3,2,1,0:T(8,128)(2,1)S(1)}, u32[]{:S(2)}, u32[]{:S(2)}) collective-permute-start(bf16[1,1,16,16]{3,2,1,0:T(8,128)(2,1)S(1)} %get-tuple-element.107), channel_id=1, source_target_pairs={{0,8},{8,16},{16,24},{24,32},{32,40},{40,48},{48,56},{56,64},{64,7... | collective-permute-start | bytes 1544 | tf_op jit(solution)/shard_map/ppermute | solution.py:25
  428.5 1.9 collective-permute-start.1
  430.4 3.0 collective-permute-done.1
  433.4 1.3 collective-permute-start.2
  434.7 1.3 collective-permute-start.3
  436.0 3.0 collective-permute-done.3
  439.4 0.8 fusion.13
  (85 shorter events, 3.3 us)
Async XLA Ops:
  7.2 319.0 %copy-start = (bf16[384,3072]{1,0:T(8,128)(2,1)S(1)}, bf16[384,3072]{1,0:T(8,128)(2,1)}, u32[]{:S(2)}) copy-start(bf16[384,3072]{1,0:T(8,128)(2,1)} %param.25) | copy-start | bytes 7077892
  7.2 169.7 %all-gather.3.cloned.1.call-start = ((), (), s32[]{:S(2)}) async-start(), calls=%async_computation.3 | async-start | bytes 3194880 | tf_op jit(solution)/shard_map/all_gather | solution.py:106
  11.4 40.0 %copy-start.5 = (bf16[1,8,1,3072]{3,1,2,0:T(8,128)(2,1)S(1)}, bf16[1,8,1,3072]{3,1,2,0:T(8,128)(2,1)}, u32[]{:S(2)}) copy-start(bf16[1,8,1,3072]{3,1,2,0:T(8,128)(2,1)} %param.20) | copy-start | bytes 147460
  51.2 247.7 %all-gather.5.cloned.1.call-start = ((), (), s32[]{:S(2)}) async-start(), calls=%async_computation.4 | async-start | bytes 3194880 | tf_op jit(solution)/shard_map/all_gather | solution.py:107
  85.2 30.4 %copy-start.13 = (s32[256]{0:T(256)S(1)}, s32[256]{0:T(256)}, u32[]{:S(2)}) copy-start(s32[256]{0:T(256)} %param.23) | copy-start | bytes 3076
  85.2 30.4 %copy-start.2 = (bf16[256,384]{1,0:T(8,128)(2,1)S(1)}, bf16[256,384]{1,0:T(8,128)(2,1)}, u32[]{:S(2)}) copy-start(bf16[256,384]{1,0:T(8,128)(2,1)} %param.21) | copy-start | bytes 589828
  88.5 27.2 %copy-start.3 = (bf16[256,384]{1,0:T(8,128)(2,1)S(1)}, bf16[256,384]{1,0:T(8,128)(2,1)}, u32[]{:S(2)}) copy-start(bf16[256,384]{1,0:T(8,128)(2,1)} %param.22) | copy-start | bytes 589828
  112.2 9.9 %all-to-all-start = ((bf16[8,2,1536]{2,1,0:T(2,128)(2,1)}), bf16[8,2,1536]{2,1,0:T(2,128)(2,1)S(1)}, u32[]{:S(2)}, u32[]{:S(2)}) async-start(bf16[8,2,1536]{2,1,0:T(2,128)(2,1)} %reshape.170), calls=%async_computation | async-start | bytes 98304 | tf_op jit(solution)/shard_map/all_to_all | solution.py:84
  115.5 303.0 %all-reduce.2.cloned.1.call-start = ((), (), s32[]{:S(2)}) async-start(), calls=%async_computation.5 | async-start | bytes 786432 | tf_op jit(solution)/shard_map/psum | solution.py:131
  326.0 1.5 copy-start.7
  326.0 92.5 %copy-start.6 = (bf16[1,8,1,3072]{3,1,2,0:T(8,128)(2,1)S(1)}, bf16[1,8,1,3072]{3,1,2,0:T(8,128)(2,1)}, u32[]{:S(2)}) copy-start(bf16[1,8,1,3072]{3,1,2,0:T(8,128)(2,1)} %param.24) | copy-start | bytes 147460
  326.1 92.5 %copy-start.8 = (f32[3072]{0:T(1024)S(1)}, f32[3072]{0:T(1024)}, u32[]{:S(2)}) copy-start(f32[3072]{0:T(1024)} %param.26) | copy-start | bytes 36868
  326.1 92.5 %copy-start.9 = (f32[3072]{0:T(1024)S(1)}, f32[3072]{0:T(1024)}, u32[]{:S(2)}) copy-start(f32[3072]{0:T(1024)} %param.27) | copy-start | bytes 36868
  326.1 93.7 %copy-start.11 = (bf16[3072,64]{0,1:T(8,128)(2,1)S(1)}, bf16[3072,64]{0,1:T(8,128)(2,1)}, u32[]{:S(2)}) copy-start(bf16[3072,64]{0,1:T(8,128)(2,1)} %param.30) | copy-start | bytes 1179652
  326.1 93.6 %copy-start.12 = (f32[3072]{0:T(1024)S(1)}, f32[3072]{0:T(1024)}, u32[]{:S(2)}) copy-start(f32[3072]{0:T(1024)} %param.28) | copy-start | bytes 36868
  326.1 93.6 %copy-start.14 = (f32[64]{0:T(128)S(1)}, f32[64]{0:T(128)}, u32[]{:S(2)}) copy-start(f32[64]{0:T(128)} %param.31) | copy-start | bytes 772
  326.1 113.2 %copy-start.1 = (bf16[3,3,3,16,512]{4,3,2,1,0:T(8,128)(2,1)S(1)}, bf16[3,3,3,16,512]{4,3,2,1,0:T(8,128)(2,1)}, u32[]{:S(2)}) copy-start(bf16[3,3,3,16,512]{4,3,2,1,0:T(8,128)(2,1)} %param.32) | copy-start | bytes 1327108
  326.1 113.2 %copy-start.10 = (f32[512]{0:T(512)S(1)}, f32[512]{0:T(512)}, u32[]{:S(2)}) copy-start(f32[512]{0:T(512)} %param.33) | copy-start | bytes 6148
  419.5 20.7 %copy-start.4 = (bf16[8,1,3072]{2,0,1:T(8,128)(2,1)}, bf16[8,1,3072]{2,0,1:T(8,128)(2,1)S(1)}, u32[]{:S(2)}) copy-start(bf16[8,1,3072]{2,0,1:T(8,128)(2,1)S(1)} %get-tuple-element.87) | copy-start | bytes 147460
  420.2 10.2 %collective-permute-start = (bf16[1,1,16,16]{3,2,1,0:T(8,128)(2,1)S(1)}, bf16[1,1,16,16]{3,2,1,0:T(8,128)(2,1)S(1)}, u32[]{:S(2)}, u32[]{:S(2)}) collective-permute-start(bf16[1,1,16,16]{3,2,1,0:T(8,128)(2,1)S(1)} %get-tuple-element.107), channel_id=1, source_target_pairs={{0,8},{8,16},{16,24},{24,32},{32,40},{40,48},{48,56},{56,64},{64,7... | collective-permute-start | bytes 1544 | tf_op jit(solution)/shard_map/ppermute | solution.py:25
  428.5 4.9 %collective-permute-start.1 = (bf16[1,1,16,16]{3,2,1,0:T(8,128)(2,1)S(1)}, bf16[1,1,16,16]{3,2,1,0:T(8,128)(2,1)S(1)}, u32[]{:S(2)}, u32[]{:S(2)}) collective-permute-start(bf16[1,1,16,16]{3,2,1,0:T(8,128)(2,1)S(1)} %get-tuple-element.108), channel_id=1, source_target_pairs={{8,0},{16,8},{24,16},{32,24},{40,32},{48,40},{56,48},{64,56},{72,6... | collective-permute-start | bytes 1544 | tf_op jit(solution)/shard_map/ppermute | solution.py:27
  433.4 2.6 collective-permute-start.2
  434.7 4.3 collective-permute-start.3
Sparse Core Ops, SparseCore 0:
  51.3 125.5 all-gather.2
  179.0 119.7 all-gather.4
  327.6 90.8 all-reduce.1
where the time goes:
time: 455 us; the launch traced here: 447 us
  waiting for transfers between devices  259 us (57%)
  local copies, waits for them, and re-layouts  61.7 us (14%)
  other arithmetic  56.6 us (12%)
  blocking collectives  23 us (5%)
  starting transfers between devices  16.4 us (4%)
  matrix products  15.2 us (3%)
  between operations  14.2 us (3%)
    all_gather x1, waiting for transfers between devices, body(): lax.all_gather(local_v, 'seq', axis=0, tiled=True)  108 us
    psum x1, waiting for transfers between devices, body(): lax.psum(partial_value.astype(jnp.bfloat16), 'head').astype(jnp.float32)  91 us
    unnamed x3, other arithmetic  54 us
    all_gather x1, waiting for transfers between devices, body(): lax.all_gather(local_k, 'seq', axis=0, tiled=True)  47.7 us
    unnamed x45, local copies, waits for them, and re-layouts  23 us
    all_to_all x1, blocking collectives, body(): lax.all_to_all(keys, 'head', split_axis=3, concat_axis=1, tiled=True)  14 us
    ppermute x2, starting transfers between devices, with_halo(): lax.ppermute(tail, axis, [(i, (i + 1) % count) for i in range(ends)])  9.52 us
  transfers between devices with their start and end apart: 8, of which 6 were waited for; matrix products, arithmetic and copies ran while one was open for 16% of the time, Pallas kernels for 0%

commit v1 on v0

v1 whole, which is shorter than its diff:
```python
import functools

import jax
import jax.numpy as jnp
from jax import lax
from jax.experimental import pallas as pl
from jax.experimental.pallas import tpu as pltpu
from jax.sharding import PartitionSpec as P

HEAD_DIM = 128
GROUP = 3
LAT_CH = 16
TOK = 8
LAYER = 4
LATENT_SCALE = 0.476986
NEG = -1e30
SCORE_SCALE = HEAD_DIM ** (-0.5)
LOG2E = 1.4426950408889634
BF16 = jnp.bfloat16
F32 = jnp.float32
MESH = pl.DeviceIdType.MESH


def dot(a, b):
    return jnp.dot(a, b, preferred_element_type=F32)


def dot_nt(a, b):
    return lax.dot_general(a, b, (((1,), (1,)), ((), ())), preferred_element_type=F32)


def kernel(
    seqs,
    heads,
    q_hbm,
    k_hbm,
    v_hbm,
    text_k_hbm,
    text_v_hbm,
    mask_hbm,
    tokens_hbm,
    out_w_hbm,
    out_bias_hbm,
    gate_hbm,
    shift_hbm,
    scale_hbm,
    final_w_hbm,
    final_bias_hbm,
    conv_w_hbm,
    conv_bias_hbm,
    block_hbm,
    decoded_hbm,
    queries,
    keys,
    values,
    text_k,
    text_v,
    mask,
    tokens,
    out_w,
    out_bias,
    gate,
    shift,
    scale,
    final_w,
    final_bias,
    conv_w,
    conv_bias,
    stage,
    landing,
    kv,
    qs,
    run_max,
    run_sum,
    run_acc,
    marks,
    o_stage,
    o_in,
    rs_stage,
    rs_in,
    lat,
    halo,
    w_sum,
    w_full,
    pixels,
    block_out,
    decoded,
    local_sem,
    out_sem,
    a2a_send,
    a2a_recv,
    ring_send,
    half_send,
    ring_recv,
    far_recv,
    q_send,
    q_recv,
    o_send,
    o_recv,
    rs_send,
    rs_recv,
    halo_send,
    halo_recv,
):
    s = lax.axis_index("seq")
    h = lax.axis_index("head")
    layers = seqs // LAYER
    far = layers // 2
    z = s // LAYER
    j = lax.rem(s, LAYER)
    width = GROUP * HEAD_DIM
    dim = heads * width
    rows = heads * TOK
    rs_parts = rs_stage.shape[0]
    part_cols = dim // rs_parts

    def shifted(index, by, count):
        return lax.rem(index + (by % count), count)

    def head_peer(i):
        return shifted(h, i, heads)

    def layer_peer(i):
        return (z * LAYER + shifted(j, i, LAYER), h)

    def slot_at(by):
        return lax.rem(z + by + layers, layers)

    right = (slot_at(1) * LAYER + j, h)
    left = (slot_at(-1) * LAYER + j, h)

    def remote(src, dst, send, recv, device):
        return pltpu.make_async_remote_copy(
            src_ref=src,
            dst_ref=dst,
            send_sem=send,
            recv_sem=recv,
            device_id=device,
            device_id_type=MESH,
        )

    pairs = (
        (k_hbm, keys),
        (v_hbm, values),
        (q_hbm, queries),
        (conv_w_hbm, conv_w),
        (text_k_hbm, text_k),
        (text_v_hbm, text_v),
        (mask_hbm, mask),
        (tokens_hbm, tokens),
        (out_w_hbm, out_w),
        (out_bias_hbm, out_bias),
        (gate_hbm, gate),
        (shift_hbm, shift),
        (scale_hbm, scale),
        (final_w_hbm, final_w),
        (final_bias_hbm, final_bias),
        (conv_bias_hbm, conv_bias),
    )
    loads = [
        pltpu.make_async_copy(src, dst, local_sem.at[i]) for i, (src, dst) in enumerate(pairs)
    ]

    halo_steps = [(dr, dc) for dr in (-1, 0, 1) for dc in (-1, 0, 1) if (dr, dc) != (0, 0)]
    halo_peers = [(shifted(s, dr, seqs), shifted(h, dc, heads)) for dr, dc in halo_steps]
    partners = [(s, head_peer(i)) for i in range(1, heads)]
    partners += [layer_peer(i) for i in range(1, LAYER)]
    partners += [right, left]
    partners += [peer for peer, (dr, dc) in zip(halo_peers, halo_steps) if dr != 0]
    for load in loads[:3]:
        load.start()
    barrier = pltpu.get_barrier_semaphore()
    for partner in partners:
        pl.semaphore_signal(barrier, inc=1, device_id=partner, device_id_type=MESH)
    for load in loads[3:]:
        load.start()
    for at, whole in enumerate((keys, values, queries)):
        loads[at].wait()
        for g in range(heads):
            stage[g, at] = whole[:, g * width : (g + 1) * width]
    pl.semaphore_wait(barrier, len(partners))

    for i in range(1, heads):
        g = head_peer(i)
        remote(stage.at[g], landing.at[h], a2a_send, a2a_recv, (s, g)).start()
    landing[h] = stage[h]

    loads[3].wait()
    conv_all = conv_w[...].astype(F32)
    taps = conv_all.shape[0] // 3
    w_sum[...] = (conv_all[:taps] + conv_all[taps : 2 * taps] + conv_all[2 * taps :]).astype(BF16)
    parities = w_full.shape[0]
    features = final_w.shape[0]

    def conv_weights(parity, carry):
        up = parity // 2
        side = lax.rem(parity, 2)
        depth = w_full.shape[1]
        row = lax.broadcasted_iota(jnp.int32, (depth, taps), 0)
        col = lax.broadcasted_iota(jnp.int32, (depth, taps), 1)
        tap_i = 2 * (row >> 7) + ((row >> 1) & 1) + up - 1
        tap_j = 2 * ((row >> 6) & 1) + (row & 1) + side - 1
        inside = (tap_i >= 0) & (tap_i <= 2) & (tap_j >= 0) & (tap_j <= 2)
        source = (tap_i * 3 + tap_j) * LAT_CH + ((row & 63) >> 2)
        pick = jnp.where(inside & (source == col), 1.0, 0.0).astype(BF16)
        w_full[parity] = dot(pick, w_sum[...]).astype(BF16)
        return carry

    lax.fori_loop(0, parities, conv_weights, 0)

    def rows_of(block):
        return block.astype(F32).reshape(rows, width).astype(BF16)

    others = landing.at[pl.ds(0, heads - 1)]
    peer = (s, head_peer(1))
    remote(others, others, a2a_send, a2a_recv, peer).wait_recv()
    own_k = rows_of(landing[:, 0])
    own_v = rows_of(landing[:, 1])
    for n in range(GROUP):
        cols = slice(n * HEAD_DIM, (n + 1) * HEAD_DIM)
        kv[z, n, 0] = own_k[:, cols]
        kv[z, n, 1] = own_v[:, cols]

    def to_right(ref, recv, send=0):
        return remote(ref, ref, ring_send.at[0] if send == 0 else half_send.at[0], recv, right)

    def to_left(ref, recv, send=0):
        return remote(ref, ref, ring_send.at[1] if send == 0 else half_send.at[1], recv, left)

    for n in range(GROUP):
        to_right(kv.at[z, n], ring_recv.at[z, n]).start()
        to_left(kv.at[z, n], ring_recv.at[z, n]).start()

    own_q = rows_of(landing[:, 2])
    for n in range(GROUP):
        qs[n, j] = own_q[:, n * HEAD_DIM : (n + 1) * HEAD_DIM]
    for i in range(1, LAYER):
        remote(qs.at[:, j], qs.at[:, j], q_send, q_recv, layer_peer(i)).start()

    def queries_of(n):
        return qs[n].reshape(LAYER * rows, HEAD_DIM)

    def attend_text(n, carry):
        cols = pl.ds(pl.multiple_of(n * HEAD_DIM, HEAD_DIM), HEAD_DIM)
        scores = dot_nt(queries_of(n), text_k[:, cols])
        count = scores.shape[1]
        lane = lax.broadcasted_iota(jnp.int32, (1, count), 1)
        share = count // LAYER
        mine = (lane >= j * share) & (lane < (j + 1) * share) & (mask[...] == 1)
        mine = jnp.broadcast_to(mine, scores.shape)
        scores = jnp.where(mine, scores, NEG)
        top = jnp.max(scores, axis=1, keepdims=True)
        weights = jnp.where(mine, jnp.exp2((scores - top) * (SCORE_SCALE * LOG2E)), 0.0)
        total = jnp.sum(weights, axis=1, keepdims=True)
        shape = run_max.shape[1:]
        run_max[n] = jnp.broadcast_to(top, shape)
        run_sum[n] = jnp.broadcast_to(total, shape)
        run_acc[n] = dot(weights.astype(BF16), text_v[:, cols])
        return carry

    def absorb(n, one, other):
        keys_now = jnp.concatenate([kv[one, n, 0], kv[other, n, 0]], axis=0)
        values_now = jnp.concatenate([kv[one, n, 1], kv[other, n, 1]], axis=0)
        scores = dot_nt(queries_of(n), keys_now)
        old = run_max[n]
        top = jnp.maximum(old, jnp.max(scores, axis=1, keepdims=True))
        factor = jnp.exp2((old - top) * (SCORE_SCALE * LOG2E))
        weights = jnp.exp2((scores - top[:, : scores.shape[1]]) * (SCORE_SCALE * LOG2E))
        total = run_sum[n] * factor + jnp.sum(weights, axis=1, keepdims=True)
        acc = run_acc[n] * factor + dot(weights.astype(BF16), values_now)
        return top, total, acc

    def pass_on(step, n):
        one = slot_at(-step)
        other = slot_at(step)
        to_right(kv.at[one, n], ring_recv.at[one, n]).wait_recv()

        @pl.when(step < far - 1)
        def _():
            to_right(kv.at[one, n], ring_recv.at[one, n]).start()

        @pl.when(step == far - 1)
        def _():
            to_right(kv.at[one, n, 0], ring_recv.at[one, n], 1).start()

        to_left(kv.at[other, n], ring_recv.at[other, n]).wait_recv()

        @pl.when(step < far - 1)
        def _():
            to_left(kv.at[other, n], ring_recv.at[other, n]).start()

        @pl.when(step == far - 1)
        def _():
            to_left(kv.at[other, n, 1], far_recv.at[n], 1).start()

    def first_step(n, carry):
        pass_on(1, n)
        return carry

    lax.fori_loop(0, GROUP, first_step, 0)
    three = qs.at[:, pl.ds(0, LAYER - 1)]
    remote(three, three, q_send, q_recv, layer_peer(1)).wait_recv()
    for load in loads[4:7]:
        load.wait()
    lax.fori_loop(0, GROUP, attend_text, 0)

    def ring_step(step, carry):
        def one_head(n, inner):
            @pl.when(step < far)
            def _():
                pass_on(step, n)

            top, total, acc = absorb(n, slot_at(1 - step), slot_at(step - 1))
            run_max[n] = top
            run_sum[n] = total
            run_acc[n] = acc
            return inner

        return lax.fori_loop(0, GROUP, one_head, carry)

    lax.fori_loop(2, far + 1, ring_step, 0)

    opposite = slot_at(far)
    lane = lax.broadcasted_iota(jnp.int32, (1, HEAD_DIM), 1)
    marks[...] = jnp.zeros_like(marks)

    def send_share(n):
        for i in range(1, LAYER):
            remote(
                o_stage.at[shifted(j, i, LAYER), n], o_in.at[j, n], o_send, o_recv, layer_peer(i)
            ).start()

    def last_step(n, carry):
        to_right(kv.at[opposite, n, 0], ring_recv.at[opposite, n]).wait_recv()
        to_left(kv.at[opposite, n, 1], far_recv.at[n]).wait_recv()
        top, total, acc = absorb(n, z, opposite)
        share = (acc / total).astype(BF16)
        for i in range(LAYER):
            o_stage[i, n] = share[i * rows : (i + 1) * rows]
        send_share(n)
        level = top * SCORE_SCALE + jnp.log(total)
        first = level.astype(BF16).astype(F32)
        second = (level - first).astype(BF16).astype(F32)
        third = level - first - second
        here = jnp.where(lane == 3 * n, first, marks[...])
        here = jnp.where(lane == 3 * n + 1, second, here)
        marks[...] = jnp.where(lane == 3 * n + 2, third, here)
        return carry

    lax.fori_loop(0, GROUP, last_step, 0)
    level_rows = marks[...].astype(BF16)
    for i in range(LAYER):
        o_stage[i, GROUP] = level_rows[i * rows : (i + 1) * rows]
    send_share(GROUP)
    o_in[j] = o_stage[j]

    for load in loads[7:]:
        load.wait()
    three = o_in.at[pl.ds(0, LAYER - 1)]
    remote(three, three, o_send, o_recv, layer_peer(1)).wait_recv()
    level_parts = [o_in[i, GROUP].astype(F32) for i in range(LAYER)]
    attended = []
    for n in range(GROUP):
        own_lanes = (lane >= 3 * n) & (lane < 3 * n + 3)
        levels = [
            jnp.sum(jnp.where(own_lanes, part, 0.0), axis=1, keepdims=True)
            for part in level_parts
        ]
        top = functools.reduce(jnp.maximum, levels)
        shares = [jnp.exp(level - top) for level in levels]
        total = functools.reduce(jnp.add, shares)
        mixed = functools.reduce(
            jnp.add, [share * o_in[i, n].astype(F32) for i, share in enumerate(shares)]
        )
        attended.append((mixed / total).astype(BF16))
    attended = jnp.concatenate(attended, axis=1)

    for part in range(rs_parts):
        product = dot(attended, out_w[:, part * part_cols : (part + 1) * part_cols])
        rs_stage[part] = product.reshape(heads, TOK, part_cols).astype(BF16)
        for i in range(1, heads):
            g = head_peer(i)
            remote(
                rs_stage.at[part, g],
                rs_in.at[part, h],
                rs_send.at[part],
                rs_recv.at[part],
                (s, g),
            ).start()
        rs_in[part, h] = rs_stage[part, h]
    pieces = []
    for part in range(rs_parts):
        cols = slice(part * part_cols, (part + 1) * part_cols)
        others = rs_in.at[part, pl.ds(0, heads - 1)]
        remote(others, others, rs_send.at[part], rs_recv.at[part], peer).wait_recv()
        projected = jnp.sum(rs_in[part].astype(F32), axis=0)
        stream = tokens[:, cols].astype(F32) + gate[:, cols] * (projected + out_bias[:, cols])
        rounded = stream.astype(BF16)
        block_out[:, cols] = rounded
        pieces.append(rounded.astype(F32))
    block_copy = pltpu.make_async_copy(block_out, block_hbm, out_sem.at[0])
    block_copy.start()

    normed_in = jnp.concatenate(pieces, axis=1)
    centered = normed_in - jnp.mean(normed_in, axis=1, keepdims=True)
    spread = jnp.mean(centered * centered, axis=1, keepdims=True)
    normed = centered * lax.rsqrt(spread + 1e-06)
    modulated = (normed * (1.0 + scale[...]) + shift[...]).astype(BF16)
    patches = (dot_nt(modulated, final_w[...]) + final_bias[...]) / LATENT_SCALE
    padded = jnp.concatenate([patches, jnp.zeros((TOK, HEAD_DIM - features), F32)], axis=1)
    lat[...] = padded.astype(BF16)

    for at, to in enumerate(halo_peers):
        remote(lat, halo.at[at], halo_send, halo_recv, to).start()
    tiles = {(0, 0): lat[...].astype(F32)}
    remote(halo, halo, halo_send, halo_recv, peer).wait_recv()
    for at, (dr, dc) in enumerate(halo_steps):
        tiles[(-dr, -dc)] = halo[at].astype(F32)

    def rolled(tile, by):
        return pltpu.roll(tile, by % HEAD_DIM, 1)

    top_edge, bottom_edge = s == 0, s == seqs - 1
    first_tile, last_tile = h == 0, h == heads - 1
    for dc in (-1, 0, 1):
        middle = tiles[(0, dc)]
        tiles[(-1, dc)] = jnp.where(top_edge, rolled(middle, 2), tiles[(-1, dc)])
        tiles[(1, dc)] = jnp.where(bottom_edge, rolled(middle, -2), tiles[(1, dc)])
    low = lane < features
    packed = {}
    for dr in (-1, 0, 1):
        middle = tiles[(dr, 0)]
        before = jnp.where(first_tile, rolled(middle, 1)[:1], tiles[(dr, -1)][TOK - 1 :])
        after = jnp.where(last_tile, rolled(middle, -1)[TOK - 1 :], tiles[(dr, 1)][:1])
        before = jnp.concatenate([before, middle[: TOK - 1]], axis=0)
        after = jnp.concatenate([middle[1:], after], axis=0)
        packed[(dr, 0)] = jnp.where(low, before, rolled(middle, features))
        packed[(dr, 1)] = jnp.where(low, middle, rolled(after, features))
    for parity in range(parities):
        up, side = parity // 2, parity % 2
        stacked = jnp.concatenate([packed[(up - 1, side)], packed[(up, side)]], axis=1)
        result = dot(stacked.astype(BF16), w_full[parity]) + conv_bias[...]
        for tile in range(pixels.shape[1]):
            pixels[up, tile, pl.ds(side, TOK, stride=2), :] = result[
                :, tile * HEAD_DIM : (tile + 1) * HEAD_DIM
            ]
    for tile in range(pixels.shape[1]):
        cols = slice(tile * HEAD_DIM, (tile + 1) * HEAD_DIM)
        decoded[:, :, cols] = pixels[:, tile].astype(BF16)
    decoded_copy = pltpu.make_async_copy(decoded, decoded_hbm, out_sem.at[1])
    decoded_copy.start()

    others = stage.at[pl.ds(0, heads - 1)]
    remote(others, others, a2a_send, a2a_recv, peer).wait_send()
    ring_all = kv.at[pl.ds(0, far - 1)]
    to_right(ring_all, far_recv.at[0]).wait_send()
    to_left(ring_all, far_recv.at[0]).wait_send()
    ring_half = kv.at[0, :, 0]
    to_right(ring_half, far_recv.at[0], 1).wait_send()
    to_left(ring_half, far_recv.at[0], 1).wait_send()
    three = qs.at[:, pl.ds(0, LAYER - 1)]
    remote(three, three, q_send, q_recv, peer).wait_send()
    three = o_stage.at[pl.ds(0, LAYER - 1)]
    remote(three, three, o_send, o_recv, peer).wait_send()
    for part in range(rs_parts):
        others = rs_stage.at[part, pl.ds(0, heads - 1)]
        remote(others, others, rs_send.at[part], rs_recv.at[part], peer).wait_send()
    remote(halo, halo, halo_send, halo_recv, peer).wait_send()
    block_copy.wait()
    decoded_copy.wait()


def hand_over(block_in, decoded_in, block_to, decoded_to, sem):
    copies = [
        pltpu.make_async_copy(block_in, block_to, sem.at[0]),
        pltpu.make_async_copy(decoded_in, decoded_to, sem.at[1]),
    ]
    for copy in copies:
        copy.start()
    for copy in copies:
        copy.wait()


def body(seqs, heads, *args):
    (
        queries,
        keys,
        values,
        text_keys,
        text_values,
        text_mask,
        tokens,
        out_weight,
        out_bias,
        gate,
        shift,
        scale,
        final_weight,
        final_bias,
        conv_weight,
        conv_bias,
    ) = args
    dim = queries.shape[3]
    width = GROUP * HEAD_DIM
    text = text_keys.shape[0]
    layers = seqs // LAYER
    far = layers // 2
    rows = heads * TOK
    features = final_weight.shape[1]
    taps = 9 * LAT_CH
    channels = conv_weight.shape[4]
    rs_parts = 2
    operands = (
        queries.reshape(TOK, dim),
        keys.reshape(TOK, dim),
        values.reshape(TOK, dim),
        text_keys,
        text_values,
        text_mask.reshape(1, text),
        tokens.reshape(TOK, dim),
        out_weight,
        out_bias.reshape(1, dim),
        gate.reshape(1, dim),
        shift.reshape(1, dim),
        scale.reshape(1, dim),
        final_weight.T,
        final_bias.reshape(1, features),
        conv_weight.reshape(3 * taps, channels),
        conv_bias.reshape(1, channels),
    )
    copied = [pltpu.VMEM(x.shape, x.dtype) for x in operands]
    dma = pltpu.SemaphoreType.DMA
    anywhere = pl.BlockSpec(memory_space=pl.ANY)
    results = (
        jax.ShapeDtypeStruct((TOK, dim), BF16),
        jax.ShapeDtypeStruct((2, 2 * TOK, channels), BF16),
    )
    block_out, decoded = pl.pallas_call(
        functools.partial(kernel, seqs, heads),
        out_shape=results,
        in_specs=[anywhere] * len(operands),
        out_specs=(anywhere, anywhere),
        scratch_shapes=copied
        + [
            pltpu.VMEM((heads, 3, TOK, width), BF16),
            pltpu.VMEM((heads, 3, TOK, width), BF16),
            pltpu.VMEM((layers, GROUP, 2, rows, HEAD_DIM), BF16),
            pltpu.VMEM((GROUP, LAYER, rows, HEAD_DIM), BF16),
            pltpu.VMEM((GROUP, LAYER * rows, HEAD_DIM), F32),
            pltpu.VMEM((GROUP, LAYER * rows, HEAD_DIM), F32),
            pltpu.VMEM((GROUP, LAYER * rows, HEAD_DIM), F32),
            pltpu.VMEM((LAYER * rows, HEAD_DIM), F32),
            pltpu.VMEM((LAYER, GROUP + 1, rows, HEAD_DIM), BF16),
            pltpu.VMEM((LAYER, GROUP + 1, rows, HEAD_DIM), BF16),
            pltpu.VMEM((rs_parts, heads, TOK, dim // rs_parts), BF16),
            pltpu.VMEM((rs_parts, heads, TOK, dim // rs_parts), BF16),
            pltpu.VMEM((TOK, HEAD_DIM), BF16),
            pltpu.VMEM((8, TOK, HEAD_DIM), BF16),
            pltpu.VMEM((taps, channels), BF16),
            pltpu.VMEM((4, 4 * features, channels), BF16),
            pltpu.VMEM((2, channels // HEAD_DIM, 2 * TOK, HEAD_DIM), F32),
            pltpu.VMEM((TOK, dim), BF16),
            pltpu.VMEM((2, 2 * TOK, channels), BF16),
            dma((len(operands),)),
            dma((2,)),
            dma,
            dma,
            dma((2,)),
            dma((2,)),
            dma((layers, GROUP)),
            dma((GROUP,)),
            dma,
            dma,
            dma,
            dma,
            dma((rs_parts,)),
            dma((rs_parts,)),
            dma,
            dma,
        ],
        compiler_params=pltpu.CompilerParams(
            collective_id=0, has_side_effects=True, vmem_limit_bytes=60 * 1024 * 1024
        ),
        cost_estimate=pl.CostEstimate(
            flops=1_200_000_000, bytes_accessed=5_000_000, transcendentals=1_000_000
        ),
    )(*operands)
    block_out, decoded = pl.pallas_call(
        hand_over,
        out_shape=results,
        in_specs=[anywhere] * 2,
        out_specs=(anywhere, anywhere),
        scratch_shapes=[dma((2,))],
        compiler_params=pltpu.CompilerParams(vmem_limit_bytes=60 * 1024 * 1024),
    )(block_out, decoded)
    return (
        block_out.reshape(1, TOK, 1, dim),
        decoded.reshape(1, 2, 2 * TOK, channels),
    )


def solution(mesh):
    seqs = mesh.shape["seq"]
    heads = mesh.shape["head"]
    spread = P("seq", "head", None, None)
    in_specs = (
        spread,
        spread,
        spread,
        P(None, "head"),
        P(None, "head"),
        P(),
        spread,
        P("head", None),
    ) + (P(),) * 8
    out_specs = (spread, P(None, "seq", "head", None))
    return jax.shard_map(
        functools.partial(body, seqs, heads),
        mesh=mesh,
        in_specs=in_specs,
        out_specs=out_specs,
        check_vma=False,
    )
```

time: 455 us -> 71.1 us (0.16); the launches traced: 447 us -> 71 us
  waiting for transfers between devices: 259 us -> 0 us
  Pallas kernels: 0 us -> 70.3 us
  local copies, waits for them, and re-layouts: 61.7 us -> 0 us
  other arithmetic: 56.6 us -> 0 us
  blocking collectives: 23 us -> 0 us
  starting transfers between devices: 16.4 us -> 0 us
  matrix products: 15.2 us -> 0 us
  between operations: 14.2 us -> 0.64 us
    all_gather x2 -> x0, waiting for transfers between devices: 156 us -> none  [the longest x1 108 us: body(): lax.all_gather(local_v, 'seq', axis=0, tiled=True)]
    psum x1 -> x0, waiting for transfers between devices: 91 us -> none  [body(): lax.psum(partial_value.astype(jnp.bfloat16), 'head').astype(jnp.float32)]
    pallas_call x0 -> x2, Pallas kernels: none -> 70.3 us  [the longest x1 66.7 us: body(): pl.pallas_call(functools.partial(kernel, seqs, heads), out_shape=results,...]
    unnamed x3 -> x0, other arithmetic: 54 us -> none
    unnamed x45 -> x0, local copies, waits for them, and re-layouts: 23 us -> none
    all_to_all x2 -> x0, blocking collectives: 23 us -> none  [the longest x1 14 us: body(): lax.all_to_all(keys, 'head', split_axis=3, concat_axis=1, tiled=True)]
    reshape x4 -> x0, local copies, waits for them, and re-layouts: 18 us -> none  [the longest x1 8.98 us: body(): all_v.reshape(count // block, block, groups, HEAD_DIM)]
    dot_general x13 -> x0, matrix products: 15.2 us -> none  [the longest x5 6.69 us: absorb(): jnp.einsum('gqe,kge->gqk', queries, block_keys, preferred_element_type=jn...]
  transfers between devices with their start and end apart: 8 -> 0, of which waited for: 6 -> 0; matrix products, arithmetic and copies ran while one was open for 16% -> 0% of each run, Pallas kernels for 0% -> 0%
where the time goes in v1:
time: 71.1 us; the launch traced here: 71 us
  Pallas kernels  70.3 us (99%)
    pallas_call x1, Pallas kernels, body(): pl.pallas_call(functools.partial(kernel, seqs, heads), out_shape=results,...  66.7 us
    pallas_call x1, Pallas kernels, body(): pl.pallas_call(hand_over, out_shape=results, in_specs=[anywhere] * 2, out...  3.6 us

profile of v1, /device:TPU:1, one launch (start us, length us, event | category | flops | bytes accessed | tf_op | source)
XLA Modules:
  0.0 71.0 jit_solution(6618533086948637288)
XLA Ops:
  0.6 66.7 %shard_map.167 = (bf16[8,3072]{1,0:T(8,128)(2,1)}, bf16[2,16,512]{2,1,0:T(8,128)(2,1)}) custom-call(bf16[8,3072]{1,0:T(8,128)(2,1)} %bitcast.17, bf16[8,3072]{1,0:T(8,128)(2,1)} %bitcast.18, bf16[8,3072]{1,0:T(8,128)(2,1)} %bitcast.19, bf16[256,384]{1,0:T(8,128)(2,1)} %text_k_hbm.1, bf16[256,384]{1,0:T(8,128)(2,1)} %text_v_hbm.1, s32[1,256]{1,0:T(1,128)} %bitcast.28, ...), custom_call_target="tpu_custom_call" | custom-call | flops 1200000000 | bytes 5000000 | tf_op jit(solution)/shard_map/pallas_call | solution.py:538
  67.4 3.6 %shard_map.168 = (bf16[8,3072]{1,0:T(8,128)(2,1)}, bf16[2,16,512]{2,1,0:T(8,128)(2,1)}) custom-call(bf16[8,3072]{1,0:T(8,128)(2,1)} %get-tuple-element.6.block_in, bf16[2,16,512]{2,1,0:T(8,128)(2,1)} %get-tuple-element.7.decoded_in), custom_call_target="tpu_custom_call" | custom-call | tf_op jit(solution)/shard_map/pallas_call | solution.py:588

commit v2 on v1

--- a/solution.py
+++ b/solution.py
@@ -117,8 +117,10 @@
     def shifted(index, by, count):
         return lax.rem(index + (by % count), count)
 
+    r = lax.rem(j + LAYER // 2, LAYER)
+
     def head_peer(i):
-        return shifted(h, i, heads)
+        return (z * LAYER + r, shifted(h, i, heads))
 
     def layer_peer(i):
         return (z * LAYER + shifted(j, i, LAYER), h)
@@ -163,10 +165,10 @@
 
     halo_steps = [(dr, dc) for dr in (-1, 0, 1) for dc in (-1, 0, 1) if (dr, dc) != (0, 0)]
     halo_peers = [(shifted(s, dr, seqs), shifted(h, dc, heads)) for dr, dc in halo_steps]
-    partners = [(s, head_peer(i)) for i in range(1, heads)]
+    partners = [head_peer(i) for i in range(heads)]
     partners += [layer_peer(i) for i in range(1, LAYER)]
     partners += [right, left]
-    partners += [peer for peer, (dr, dc) in zip(halo_peers, halo_steps) if dr != 0]
+    partners += halo_peers
     for load in loads[:3]:
         load.start()
     barrier = pltpu.get_barrier_semaphore()
@@ -180,10 +182,9 @@
             stage[g, at] = whole[:, g * width : (g + 1) * width]
     pl.semaphore_wait(barrier, len(partners))
 
-    for i in range(1, heads):
-        g = head_peer(i)
-        remote(stage.at[g], landing.at[h], a2a_send, a2a_recv, (s, g)).start()
-    landing[h] = stage[h]
+    for i in range(heads):
+        peer = head_peer(i)
+        remote(stage.at[peer[1]], landing.at[h], a2a_send, a2a_recv, peer).start()
 
     loads[3].wait()
     conv_all = conv_w[...].astype(F32)
@@ -211,9 +212,8 @@
     def rows_of(block):
         return block.astype(F32).reshape(rows, width).astype(BF16)
 
-    others = landing.at[pl.ds(0, heads - 1)]
-    peer = (s, head_peer(1))
-    remote(others, others, a2a_send, a2a_recv, peer).wait_recv()
+    peer = head_peer(0)
+    remote(landing, landing, a2a_send, a2a_recv, peer).wait_recv()
     own_k = rows_of(landing[:, 0])
     own_v = rows_of(landing[:, 1])
     for n in range(GROUP):
@@ -233,9 +233,9 @@
 
     own_q = rows_of(landing[:, 2])
     for n in range(GROUP):
-        qs[n, j] = own_q[:, n * HEAD_DIM : (n + 1) * HEAD_DIM]
+        qs[n, r] = own_q[:, n * HEAD_DIM : (n + 1) * HEAD_DIM]
     for i in range(1, LAYER):
-        remote(qs.at[:, j], qs.at[:, j], q_send, q_recv, layer_peer(i)).start()
+        remote(qs.at[:, r], qs.at[:, r], q_send, q_recv, layer_peer(i)).start()
 
     def queries_of(n):
         return qs[n].reshape(LAYER * rows, HEAD_DIM)
@@ -306,17 +306,19 @@
 
     def ring_step(step, carry):
         def one_head(n, inner):
-            @pl.when(step < far)
-            def _():
-                pass_on(step, n)
-
-            top, total, acc = absorb(n, slot_at(1 - step), slot_at(step - 1))
+            pass_on(step, n)
+            return inner
+
+        @pl.when(step < far)
+        def _():
+            lax.fori_loop(0, GROUP, one_head, 0)
+
+        news = [absorb(n, slot_at(1 - step), slot_at(step - 1)) for n in range(GROUP)]
+        for n, (top, total, acc) in enumerate(news):
             run_max[n] = top
             run_sum[n] = total
             run_acc[n] = acc
-            return inner
-
-        return lax.fori_loop(0, GROUP, one_head, carry)
+        return carry
 
     lax.fori_loop(2, far + 1, ring_step, 0)
 
@@ -327,7 +329,7 @@
     def send_share(n):
         for i in range(1, LAYER):
             remote(
-                o_stage.at[shifted(j, i, LAYER), n], o_in.at[j, n], o_send, o_recv, layer_peer(i)
+                o_stage.at[shifted(r, i, LAYER), n], o_in.at[j, n], o_send, o_recv, layer_peer(i)
             ).start()
 
     def last_step(n, carry):
@@ -352,7 +354,7 @@
     for i in range(LAYER):
         o_stage[i, GROUP] = level_rows[i * rows : (i + 1) * rows]
     send_share(GROUP)
-    o_in[j] = o_stage[j]
+    o_in[j] = o_stage[r]
 
     for load in loads[7:]:
         load.wait()
@@ -378,21 +380,20 @@
     for part in range(rs_parts):
         product = dot(attended, out_w[:, part * part_cols : (part + 1) * part_cols])
         rs_stage[part] = product.reshape(heads, TOK, part_cols).astype(BF16)
-        for i in range(1, heads):
-            g = head_peer(i)
+        for i in range(heads):
+            to = head_peer(i)
             remote(
-                rs_stage.at[part, g],
+                rs_stage.at[part, to[1]],
                 rs_in.at[part, h],
                 rs_send.at[part],
                 rs_recv.at[part],
-                (s, g),
+                to,
             ).start()
-        rs_in[part, h] = rs_stage[part, h]
     pieces = []
     for part in range(rs_parts):
         cols = slice(part * part_cols, (part + 1) * part_cols)
-        others = rs_in.at[part, pl.ds(0, heads - 1)]
-        remote(others, others, rs_send.at[part], rs_recv.at[part], peer).wait_recv()
+        whole = rs_in.at[part]
+        remote(whole, whole, rs_send.at[part], rs_recv.at[part], peer).wait_recv()
         projected = jnp.sum(rs_in[part].astype(F32), axis=0)
         stream = tokens[:, cols].astype(F32) + gate[:, cols] * (projected + out_bias[:, cols])
         rounded = stream.astype(BF16)
@@ -450,8 +451,7 @@
     decoded_copy = pltpu.make_async_copy(decoded, decoded_hbm, out_sem.at[1])
     decoded_copy.start()
 
-    others = stage.at[pl.ds(0, heads - 1)]
-    remote(others, others, a2a_send, a2a_recv, peer).wait_send()
+    remote(stage, stage, a2a_send, a2a_recv, peer).wait_send()
     ring_all = kv.at[pl.ds(0, far - 1)]
     to_right(ring_all, far_recv.at[0]).wait_send()
     to_left(ring_all, far_recv.at[0]).wait_send()
@@ -463,22 +463,11 @@
     three = o_stage.at[pl.ds(0, LAYER - 1)]
     remote(three, three, o_send, o_recv, peer).wait_send()
     for part in range(rs_parts):
-        others = rs_stage.at[part, pl.ds(0, heads - 1)]
-        remote(others, others, rs_send.at[part], rs_recv.at[part], peer).wait_send()
+        whole = rs_stage.at[part]
+        remote(whole, whole, rs_send.at[part], rs_recv.at[part], peer).wait_send()
     remote(halo, halo, halo_send, halo_recv, peer).wait_send()
     block_copy.wait()
     decoded_copy.wait()
-
-
-def hand_over(block_in, decoded_in, block_to, decoded_to, sem):
-    copies = [
-        pltpu.make_async_copy(block_in, block_to, sem.at[0]),
-        pltpu.make_async_copy(decoded_in, decoded_to, sem.at[1]),
-    ]
-    for copy in copies:
-        copy.start()
-    for copy in copies:
-        copy.wait()
 
 
 def body(seqs, heads, *args):
@@ -585,14 +574,6 @@
             flops=1_200_000_000, bytes_accessed=5_000_000, transcendentals=1_000_000
         ),
     )(*operands)
-    block_out, decoded = pl.pallas_call(
-        hand_over,
-        out_shape=results,
-        in_specs=[anywhere] * 2,
-        out_specs=(anywhere, anywhere),
-        scratch_shapes=[dma((2,))],
-        compiler_params=pltpu.CompilerParams(vmem_limit_bytes=60 * 1024 * 1024),
-    )(block_out, decoded)
     return (
         block_out.reshape(1, TOK, 1, dim),
         decoded.reshape(1, 2, 2 * TOK, channels),

time: 71.1 us -> 68.8 us (0.968)
  Pallas kernels: 70.3 us -> 65.1 us
  local copies, waits for them, and re-layouts: 0 us -> 2.8 us
    pallas_call x1 -> x0, Pallas kernels: 3.6 us -> none  [body(): pl.pallas_call(hand_over, out_shape=results, in_specs=[anywhere] * 2, out...]
    unnamed x0 -> x2, local copies, waits for them, and re-layouts: none -> 2.8 us
    pallas_call x1, Pallas kernels: 66.7 us -> 65.1 us  [body(): pl.pallas_call(functools.partial(kernel, seqs, heads), out_shape=results,...]
where the time goes in v2:
time: 68.8 us; the launch traced here: 68.5 us
  Pallas kernels  65.1 us (95%)
  local copies, waits for them, and re-layouts  2.8 us (4%)
    pallas_call x1, Pallas kernels, body(): pl.pallas_call(functools.partial(kernel, seqs, heads), out_shape=results,...  65.1 us
    unnamed x2, local copies, waits for them, and re-layouts  2.8 us

profile of v2, /device:TPU:1, one launch (start us, length us, event | category | flops | bytes accessed | tf_op | source)
XLA Modules:
  0.0 68.5 jit_solution(7482372370699230996)
XLA Ops:
  0.6 65.1 %shard_map.167 = (bf16[8,3072]{1,0:T(8,128)(2,1)}, bf16[2,16,512]{2,1,0:T(8,128)(2,1)}) custom-call(bf16[8,3072]{1,0:T(8,128)(2,1)} %bitcast.19, bf16[8,3072]{1,0:T(8,128)(2,1)} %bitcast.20, bf16[8,3072]{1,0:T(8,128)(2,1)} %bitcast.21, bf16[256,384]{1,0:T(8,128)(2,1)} %text_k_hbm.1, bf16[256,384]{1,0:T(8,128)(2,1)} %text_v_hbm.1, s32[1,256]{1,0:T(1,128)} %bitcast.28, ...), custom_call_target="tpu_custom_call" | custom-call | flops 1200000000 | bytes 5000000 | tf_op jit(solution)/shard_map/pallas_call | solution.py:527
  65.7 1.4 %copy.20 = bf16[1,8,1,3072]{3,1,2,0:T(8,128)(2,1)} copy(bf16[1,8,1,3072]{3,1,2,0:T(8,128)(2,1)} %bitcast.15) | data formatting | bytes 98304
  67.2 1.4 %copy.21 = bf16[1,2,16,512]{3,2,1,0:T(8,128)(2,1)} copy(bf16[1,2,16,512]{3,2,1,0:T(8,128)(2,1)} %bitcast.16) | data formatting | bytes 65536

commit v3 on v2

--- a/solution.py
+++ b/solution.py
@@ -23,6 +23,10 @@
 
 def dot(a, b):
     return jnp.dot(a, b, preferred_element_type=F32)
+
+
+def dot_tn(a, b):
+    return lax.dot_general(a, b, (((0,), (0,)), ((), ())), preferred_element_type=F32)
 
 
 def dot_nt(a, b):
@@ -66,14 +70,21 @@
     final_bias,
     conv_w,
     conv_bias,
-    stage,
-    landing,
+    kv_stage,
+    q_stage,
+    kv_in,
+    q_in,
     kv,
     qs,
+    q_turned,
+    mask_column,
     run_max,
     run_sum,
     run_acc,
     marks,
+    mark_stage,
+    mark_in,
+    shares,
     o_stage,
     o_in,
     rs_stage,
@@ -87,8 +98,10 @@
     decoded,
     local_sem,
     out_sem,
-    a2a_send,
-    a2a_recv,
+    kv_send,
+    kv_recv,
+    q_a2a_send,
+    q_a2a_recv,
     ring_send,
     half_send,
     ring_recv,
@@ -97,6 +110,8 @@
     q_recv,
     o_send,
     o_recv,
+    mark_send,
+    mark_recv,
     rs_send,
     rs_recv,
     halo_send,
@@ -174,26 +189,92 @@
     barrier = pltpu.get_barrier_semaphore()
     for partner in partners:
         pl.semaphore_signal(barrier, inc=1, device_id=partner, device_id_type=MESH)
-    for load in loads[3:]:
-        load.start()
-    for at, whole in enumerate((keys, values, queries)):
+    group_cols = [slice(g * width, (g + 1) * width) for g in range(heads)]
+    for at, whole in enumerate((keys, values)):
         loads[at].wait()
-        for g in range(heads):
-            stage[g, at] = whole[:, g * width : (g + 1) * width]
+        for g, cols in enumerate(group_cols):
+            kv_stage[g, at] = whole[:, cols]
     pl.semaphore_wait(barrier, len(partners))
 
     for i in range(heads):
         peer = head_peer(i)
-        remote(stage.at[peer[1]], landing.at[h], a2a_send, a2a_recv, peer).start()
-
-    loads[3].wait()
-    conv_all = conv_w[...].astype(F32)
-    taps = conv_all.shape[0] // 3
-    w_sum[...] = (conv_all[:taps] + conv_all[taps : 2 * taps] + conv_all[2 * taps :]).astype(BF16)
+        remote(kv_stage.at[peer[1]], kv_in.at[h], kv_send, kv_recv, peer).start()
+    loads[2].wait()
+    for g, cols in enumerate(group_cols):
+        q_stage[g] = queries[:, cols]
+    for i in range(heads):
+        peer = head_peer(i)
+        remote(q_stage.at[peer[1]], q_in.at[h], q_a2a_send, q_a2a_recv, peer).start()
+    for load in loads[3:7]:
+        load.start()
+
+    def rows_of(block):
+        return block.astype(F32).reshape(rows, width).astype(BF16)
+
+    peer = head_peer(0)
+    remote(kv_in, kv_in, kv_send, kv_recv, peer).wait_recv()
+    own_k = rows_of(kv_in[:, 0])
+    own_v = rows_of(kv_in[:, 1])
+    for n in range(GROUP):
+        cols = slice(n * HEAD_DIM, (n + 1) * HEAD_DIM)
+        kv[z, n, 0] = own_k[:, cols]
+        kv[z, n, 1] = own_v[:, cols]
+
+    def to_right(ref, recv, send=0):
+        return remote(ref, ref, ring_send.at[0] if send == 0 else half_send.at[0], recv, right)
+
+    def to_left(ref, recv, send=0):
+        return remote(ref, ref, ring_send.at[1] if send == 0 else half_send.at[1], recv, left)
+
+    for n in range(GROUP):
+        to_right(kv.at[z, n], ring_recv.at[z, n]).start()
+        to_left(kv.at[z, n], ring_recv.at[z, n]).start()
+
+    for load in loads[7:]:
+        load.start()
+
+    remote(q_in, q_in, q_a2a_send, q_a2a_recv, peer).wait_recv()
+    own_q = rows_of(q_in[...])
+    for n in range(GROUP):
+        qs[n, r] = own_q[:, n * HEAD_DIM : (n + 1) * HEAD_DIM]
+    for i in range(1, LAYER):
+        remote(qs.at[:, r], qs.at[:, r], q_send, q_recv, layer_peer(i)).start()
+
+    def attend_text(n):
+        share = text_k.shape[0] // LAYER
+        mine = pl.ds(pl.multiple_of(j * share, share), share)
+        cols = slice(n * HEAD_DIM, (n + 1) * HEAD_DIM)
+        scores = dot(text_k[mine, cols], q_turned[n])
+        real = jnp.broadcast_to(mask_column[mine, :1] == 1.0, scores.shape)
+        scores = jnp.where(real, scores, NEG)
+        top = jnp.max(scores, axis=0, keepdims=True)
+        weights = jnp.where(real, jnp.exp2((scores - top) * (SCORE_SCALE * LOG2E)), 0.0)
+        run_max[n, :1] = top
+        run_sum[n, :1] = jnp.sum(weights, axis=0, keepdims=True)
+        run_acc[n] = dot_tn(text_v[mine, cols], weights.astype(BF16))
+
+    def absorb(n, one, other):
+        keys_now = jnp.concatenate([kv[one, n, 0], kv[other, n, 0]], axis=0)
+        values_now = jnp.concatenate([kv[one, n, 1], kv[other, n, 1]], axis=0)
+        scores = dot(keys_now, q_turned[n])
+        old = run_max[n, :1]
+        top = jnp.maximum(old, jnp.max(scores, axis=0, keepdims=True))
+        factor = jnp.exp2((old - top) * (SCORE_SCALE * LOG2E))
+        weights = jnp.exp2((scores - top) * (SCORE_SCALE * LOG2E))
+        total = run_sum[n, :1] * factor + jnp.sum(weights, axis=0, keepdims=True)
+        acc = run_acc[n] * factor + dot_tn(values_now, weights.astype(BF16))
+        return top, total, acc
+
+    taps = w_sum.shape[0]
     parities = w_full.shape[0]
     features = final_w.shape[0]
 
-    def conv_weights(parity, carry):
+    def sum_taps():
+        conv_all = conv_w[...].astype(F32)
+        total = conv_all[:taps] + conv_all[taps : 2 * taps] + conv_all[2 * taps :]
+        w_sum[...] = total.astype(BF16)
+
+    def conv_weights(parity):
         up = parity // 2
         side = lax.rem(parity, 2)
         depth = w_full.shape[1]
@@ -205,176 +286,130 @@
         source = (tap_i * 3 + tap_j) * LAT_CH + ((row & 63) >> 2)
         pick = jnp.where(inside & (source == col), 1.0, 0.0).astype(BF16)
         w_full[parity] = dot(pick, w_sum[...]).astype(BF16)
-        return carry
-
-    lax.fori_loop(0, parities, conv_weights, 0)
-
-    def rows_of(block):
-        return block.astype(F32).reshape(rows, width).astype(BF16)
-
-    peer = head_peer(0)
-    remote(landing, landing, a2a_send, a2a_recv, peer).wait_recv()
-    own_k = rows_of(landing[:, 0])
-    own_v = rows_of(landing[:, 1])
-    for n in range(GROUP):
-        cols = slice(n * HEAD_DIM, (n + 1) * HEAD_DIM)
-        kv[z, n, 0] = own_k[:, cols]
-        kv[z, n, 1] = own_v[:, cols]
-
-    def to_right(ref, recv, send=0):
-        return remote(ref, ref, ring_send.at[0] if send == 0 else half_send.at[0], recv, right)
-
-    def to_left(ref, recv, send=0):
-        return remote(ref, ref, ring_send.at[1] if send == 0 else half_send.at[1], recv, left)
-
-    for n in range(GROUP):
-        to_right(kv.at[z, n], ring_recv.at[z, n]).start()
-        to_left(kv.at[z, n], ring_recv.at[z, n]).start()
-
-    own_q = rows_of(landing[:, 2])
-    for n in range(GROUP):
-        qs[n, r] = own_q[:, n * HEAD_DIM : (n + 1) * HEAD_DIM]
-    for i in range(1, LAYER):
-        remote(qs.at[:, r], qs.at[:, r], q_send, q_recv, layer_peer(i)).start()
-
-    def queries_of(n):
-        return qs[n].reshape(LAYER * rows, HEAD_DIM)
-
-    def attend_text(n, carry):
-        cols = pl.ds(pl.multiple_of(n * HEAD_DIM, HEAD_DIM), HEAD_DIM)
-        scores = dot_nt(queries_of(n), text_k[:, cols])
-        count = scores.shape[1]
-        lane = lax.broadcasted_iota(jnp.int32, (1, count), 1)
-        share = count // LAYER
-        mine = (lane >= j * share) & (lane < (j + 1) * share) & (mask[...] == 1)
-        mine = jnp.broadcast_to(mine, scores.shape)
-        scores = jnp.where(mine, scores, NEG)
-        top = jnp.max(scores, axis=1, keepdims=True)
-        weights = jnp.where(mine, jnp.exp2((scores - top) * (SCORE_SCALE * LOG2E)), 0.0)
-        total = jnp.sum(weights, axis=1, keepdims=True)
-        shape = run_max.shape[1:]
-        run_max[n] = jnp.broadcast_to(top, shape)
-        run_sum[n] = jnp.broadcast_to(total, shape)
-        run_acc[n] = dot(weights.astype(BF16), text_v[:, cols])
-        return carry
-
-    def absorb(n, one, other):
-        keys_now = jnp.concatenate([kv[one, n, 0], kv[other, n, 0]], axis=0)
-        values_now = jnp.concatenate([kv[one, n, 1], kv[other, n, 1]], axis=0)
-        scores = dot_nt(queries_of(n), keys_now)
-        old = run_max[n]
-        top = jnp.maximum(old, jnp.max(scores, axis=1, keepdims=True))
-        factor = jnp.exp2((old - top) * (SCORE_SCALE * LOG2E))
-        weights = jnp.exp2((scores - top[:, : scores.shape[1]]) * (SCORE_SCALE * LOG2E))
-        total = run_sum[n] * factor + jnp.sum(weights, axis=1, keepdims=True)
-        acc = run_acc[n] * factor + dot(weights.astype(BF16), values_now)
-        return top, total, acc
-
-    def pass_on(step, n):
+
+    def pass_on(step):
         one = slot_at(-step)
         other = slot_at(step)
-        to_right(kv.at[one, n], ring_recv.at[one, n]).wait_recv()
-
+        for n in range(GROUP):
+            to_right(kv.at[one, n], ring_recv.at[one, n]).wait_recv()
+            to_right(kv.at[one, n], ring_recv.at[one, n]).start()
+            to_left(kv.at[other, n], ring_recv.at[other, n]).wait_recv()
+            to_left(kv.at[other, n], ring_recv.at[other, n]).start()
+
+    def pass_on_halves(step):
+        one = slot_at(-step)
+        other = slot_at(step)
+        for n in range(GROUP):
+            to_right(kv.at[one, n], ring_recv.at[one, n]).wait_recv()
+            to_right(kv.at[one, n, 0], ring_recv.at[one, n], 1).start()
+            to_left(kv.at[other, n], ring_recv.at[other, n]).wait_recv()
+            to_left(kv.at[other, n, 1], far_recv.at[n], 1).start()
+
+    pass_on(1)
+    three = qs.at[:, pl.ds(0, LAYER - 1)]
+    remote(three, three, q_send, q_recv, layer_peer(1)).wait_recv()
+    for n in range(GROUP):
+        q_turned[n] = qs[n].reshape(LAYER * rows, HEAD_DIM).T
+    for load in loads[3:7]:
+        load.wait()
+    mask_column[...] = jnp.broadcast_to(mask[...].astype(F32), (TOK, mask.shape[1])).T
+    for n in range(GROUP):
+        attend_text(n)
+    sum_taps()
+    in_loop = min(parities, max(0, far - 3))
+
+    def ring_step(step, carry):
         @pl.when(step < far - 1)
         def _():
-            to_right(kv.at[one, n], ring_recv.at[one, n]).start()
+            pass_on(step)
 
         @pl.when(step == far - 1)
         def _():
-            to_right(kv.at[one, n, 0], ring_recv.at[one, n], 1).start()
-
-        to_left(kv.at[other, n], ring_recv.at[other, n]).wait_recv()
-
-        @pl.when(step < far - 1)
-        def _():
-            to_left(kv.at[other, n], ring_recv.at[other, n]).start()
-
-        @pl.when(step == far - 1)
-        def _():
-            to_left(kv.at[other, n, 1], far_recv.at[n], 1).start()
-
-    def first_step(n, carry):
-        pass_on(1, n)
-        return carry
-
-    lax.fori_loop(0, GROUP, first_step, 0)
-    three = qs.at[:, pl.ds(0, LAYER - 1)]
-    remote(three, three, q_send, q_recv, layer_peer(1)).wait_recv()
-    for load in loads[4:7]:
-        load.wait()
-    lax.fori_loop(0, GROUP, attend_text, 0)
-
-    def ring_step(step, carry):
-        def one_head(n, inner):
-            pass_on(step, n)
-            return inner
-
-        @pl.when(step < far)
-        def _():
-            lax.fori_loop(0, GROUP, one_head, 0)
+            pass_on_halves(step)
 
         news = [absorb(n, slot_at(1 - step), slot_at(step - 1)) for n in range(GROUP)]
         for n, (top, total, acc) in enumerate(news):
-            run_max[n] = top
-            run_sum[n] = total
+            run_max[n, :1] = top
+            run_sum[n, :1] = total
             run_acc[n] = acc
+
+        @pl.when(step - 2 < in_loop)
+        def _():
+            conv_weights(step - 2)
+
         return carry
 
     lax.fori_loop(2, far + 1, ring_step, 0)
+    for parity in range(in_loop, parities):
+        conv_weights(jnp.int32(parity))
 
     opposite = slot_at(far)
-    lane = lax.broadcasted_iota(jnp.int32, (1, HEAD_DIM), 1)
     marks[...] = jnp.zeros_like(marks)
 
-    def send_share(n):
-        for i in range(1, LAYER):
-            remote(
-                o_stage.at[shifted(r, i, LAYER), n], o_in.at[j, n], o_send, o_recv, layer_peer(i)
-            ).start()
+    def share_of(i):
+        return shifted(r, i, LAYER)
 
     def last_step(n, carry):
         to_right(kv.at[opposite, n, 0], ring_recv.at[opposite, n]).wait_recv()
         to_left(kv.at[opposite, n, 1], far_recv.at[n]).wait_recv()
         top, total, acc = absorb(n, z, opposite)
-        share = (acc / total).astype(BF16)
+        share = (acc / total).T.astype(BF16)
         for i in range(LAYER):
             o_stage[i, n] = share[i * rows : (i + 1) * rows]
-        send_share(n)
+        for i in range(1, LAYER):
+            remote(
+                o_stage.at[share_of(i), n], o_in.at[j, n], o_send, o_recv, layer_peer(i)
+            ).start()
         level = top * SCORE_SCALE + jnp.log(total)
         first = level.astype(BF16).astype(F32)
         second = (level - first).astype(BF16).astype(F32)
-        third = level - first - second
-        here = jnp.where(lane == 3 * n, first, marks[...])
-        here = jnp.where(lane == 3 * n + 1, second, here)
-        marks[...] = jnp.where(lane == 3 * n + 2, third, here)
+        marks[pl.ds(3 * n, 1)] = first
+        marks[pl.ds(3 * n + 1, 1)] = second
+        marks[pl.ds(3 * n + 2, 1)] = level - first - second
         return carry
 
     lax.fori_loop(0, GROUP, last_step, 0)
-    level_rows = marks[...].astype(BF16)
+    level_rows = marks[...]
+    lanes = mark_stage.shape[2]
     for i in range(LAYER):
-        o_stage[i, GROUP] = level_rows[i * rows : (i + 1) * rows]
-    send_share(GROUP)
+        turned = level_rows if i == 0 else pltpu.roll(level_rows, (LAYER - i) * rows, 1)
+        mark_stage[i] = turned[:, :lanes].astype(BF16)
+    for i in range(1, LAYER):
+        remote(
+            mark_stage.at[share_of(i)], mark_in.at[j], mark_send, mark_recv, layer_peer(i)
+        ).start()
     o_in[j] = o_stage[r]
+    mark_in[j] = mark_stage[r]
 
     for load in loads[7:]:
         load.wait()
     three = o_in.at[pl.ds(0, LAYER - 1)]
     remote(three, three, o_send, o_recv, layer_peer(1)).wait_recv()
-    level_parts = [o_in[i, GROUP].astype(F32) for i in range(LAYER)]
-    attended = []
+    three = mark_in.at[pl.ds(0, LAYER - 1)]
+    remote(three, three, mark_send, mark_recv, layer_peer(1)).wait_recv()
+    level_parts = [mark_in[i].astype(F32) for i in range(LAYER)]
+    shares[...] = jnp.zeros_like(shares)
     for n in range(GROUP):
-        own_lanes = (lane >= 3 * n) & (lane < 3 * n + 3)
         levels = [
-            jnp.sum(jnp.where(own_lanes, part, 0.0), axis=1, keepdims=True)
+            part[3 * n : 3 * n + 1] + part[3 * n + 1 : 3 * n + 2] + part[3 * n + 2 : 3 * n + 3]
             for part in level_parts
         ]
         top = functools.reduce(jnp.maximum, levels)
-        shares = [jnp.exp(level - top) for level in levels]
-        total = functools.reduce(jnp.add, shares)
+        parts = [jnp.exp(level - top) for level in levels]
+        total = functools.reduce(jnp.add, parts)
+        for i, part in enumerate(parts):
+            shares[n * LAYER + i : n * LAYER + i + 1] = part / total
+    columns = shares[...].T[:rows]
+    attended = []
+    for n in range(GROUP):
         mixed = functools.reduce(
-            jnp.add, [share * o_in[i, n].astype(F32) for i, share in enumerate(shares)]
+            jnp.add,
+            [
+                columns[:, n * LAYER + i : n * LAYER + i + 1] * o_in[i, n].astype(F32)
+                for i in range(LAYER)
+            ],
         )
-        attended.append((mixed / total).astype(BF16))
+        attended.append(mixed.astype(BF16))
     attended = jnp.concatenate(attended, axis=1)
 
     for part in range(rs_parts):
@@ -427,7 +462,7 @@
         middle = tiles[(0, dc)]
         tiles[(-1, dc)] = jnp.where(top_edge, rolled(middle, 2), tiles[(-1, dc)])
         tiles[(1, dc)] = jnp.where(bottom_edge, rolled(middle, -2), tiles[(1, dc)])
-    low = lane < features
+    low = lax.broadcasted_iota(jnp.int32, (1, HEAD_DIM), 1) < features
     packed = {}
     for dr in (-1, 0, 1):
         middle = tiles[(dr, 0)]
@@ -451,7 +486,8 @@
     decoded_copy = pltpu.make_async_copy(decoded, decoded_hbm, out_sem.at[1])
     decoded_copy.start()
 
-    remote(stage, stage, a2a_send, a2a_recv, peer).wait_send()
+    remote(kv_stage, kv_stage, kv_send, kv_recv, peer).wait_send()
+    remote(q_stage, q_stage, q_a2a_send, q_a2a_recv, peer).wait_send()
     ring_all = kv.at[pl.ds(0, far - 1)]
     to_right(ring_all, far_recv.at[0]).wait_send()
     to_left(ring_all, far_recv.at[0]).wait_send()
@@ -462,6 +498,8 @@
     remote(three, three, q_send, q_recv, peer).wait_send()
     three = o_stage.at[pl.ds(0, LAYER - 1)]
     remote(three, three, o_send, o_recv, peer).wait_send()
+    three = mark_stage.at[pl.ds(0, LAYER - 1)]
+    remote(three, three, mark_send, mark_recv, peer).wait_send()
     for part in range(rs_parts):
         whole = rs_stage.at[part]
         remote(whole, whole, rs_send.at[part], rs_recv.at[part], peer).wait_send()
@@ -531,16 +569,23 @@
         out_specs=(anywhere, anywhere),
         scratch_shapes=copied
         + [
-            pltpu.VMEM((heads, 3, TOK, width), BF16),
-            pltpu.VMEM((heads, 3, TOK, width), BF16),
+            pltpu.VMEM((heads, 2, TOK, width), BF16),
+            pltpu.VMEM((heads, TOK, width), BF16),
+            pltpu.VMEM((heads, 2, TOK, width), BF16),
+            pltpu.VMEM((heads, TOK, width), BF16),
             pltpu.VMEM((layers, GROUP, 2, rows, HEAD_DIM), BF16),
             pltpu.VMEM((GROUP, LAYER, rows, HEAD_DIM), BF16),
-            pltpu.VMEM((GROUP, LAYER * rows, HEAD_DIM), F32),
-            pltpu.VMEM((GROUP, LAYER * rows, HEAD_DIM), F32),
-            pltpu.VMEM((GROUP, LAYER * rows, HEAD_DIM), F32),
-            pltpu.VMEM((LAYER * rows, HEAD_DIM), F32),
-            pltpu.VMEM((LAYER, GROUP + 1, rows, HEAD_DIM), BF16),
-            pltpu.VMEM((LAYER, GROUP + 1, rows, HEAD_DIM), BF16),
+            pltpu.VMEM((GROUP, HEAD_DIM, LAYER * rows), BF16),
+            pltpu.VMEM((text, TOK), F32),
+            pltpu.VMEM((GROUP, TOK, LAYER * rows), F32),
+            pltpu.VMEM((GROUP, TOK, LAYER * rows), F32),
+            pltpu.VMEM((GROUP, HEAD_DIM, LAYER * rows), F32),
+            pltpu.VMEM((16, LAYER * rows), F32),
+            pltpu.VMEM((LAYER, 16, min(HEAD_DIM, LAYER * rows)), BF16),
+            pltpu.VMEM((LAYER, 16, min(HEAD_DIM, LAYER * rows)), BF16),
+            pltpu.VMEM((16, min(HEAD_DIM, LAYER * rows)), F32),
+            pltpu.VMEM((LAYER, GROUP, rows, HEAD_DIM), BF16),
+            pltpu.VMEM((LAYER, GROUP, rows, HEAD_DIM), BF16),
             pltpu.VMEM((rs_parts, heads, TOK, dim // rs_parts), BF16),
             pltpu.VMEM((rs_parts, heads, TOK, dim // rs_parts), BF16),
             pltpu.VMEM((TOK, HEAD_DIM), BF16),
@@ -554,10 +599,14 @@
             dma((2,)),
             dma,
             dma,
+            dma,
+            dma,
             dma((2,)),
             dma((2,)),
             dma((layers, GROUP)),
             dma((GROUP,)),
+            dma,
+            dma,
             dma,
             dma,
             dma,

time: 68.8 us -> 69.1 us (level)
  no operation moved by 1% of the time
where the time goes in v3:
time: 69.1 us; the launch traced here: 68.8 us
  Pallas kernels  65.4 us (95%)
  local copies, waits for them, and re-layouts  2.8 us (4%)
    pallas_call x1, Pallas kernels, body(): pl.pallas_call(functools.partial(kernel, seqs, heads), out_shape=results,...  65.4 us
    unnamed x2, local copies, waits for them, and re-layouts  2.8 us

profile of v3, /device:TPU:1, one launch (start us, length us, event | category | flops | bytes accessed | tf_op | source)
XLA Modules:
  0.0 68.8 jit_solution(14812367835844469675)
XLA Ops:
  0.6 65.4 %shard_map.167 = (bf16[8,3072]{1,0:T(8,128)(2,1)}, bf16[2,16,512]{2,1,0:T(8,128)(2,1)}) custom-call(bf16[8,3072]{1,0:T(8,128)(2,1)} %bitcast.19, bf16[8,3072]{1,0:T(8,128)(2,1)} %bitcast.20, bf16[8,3072]{1,0:T(8,128)(2,1)} %bitcast.21, bf16[256,384]{1,0:T(8,128)(2,1)} %text_k_hbm.1, bf16[256,384]{1,0:T(8,128)(2,1)} %text_v_hbm.1, s32[1,256]{1,0:T(1,128)} %bitcast.28, ...), custom_call_target="tpu_custom_call" | custom-call | flops 1200000000 | bytes 5000000 | tf_op jit(solution)/shard_map/pallas_call | solution.py:565
  66.0 1.4 %copy.20 = bf16[1,8,1,3072]{3,1,2,0:T(8,128)(2,1)} copy(bf16[1,8,1,3072]{3,1,2,0:T(8,128)(2,1)} %bitcast.15) | data formatting | bytes 98304
  67.4 1.4 %copy.21 = bf16[1,2,16,512]{3,2,1,0:T(8,128)(2,1)} copy(bf16[1,2,16,512]{3,2,1,0:T(8,128)(2,1)} %bitcast.16) | data formatting | bytes 65536

commit v4 on v3

--- a/solution.py
+++ b/solution.py
@@ -105,7 +105,6 @@
     ring_send,
     half_send,
     ring_recv,
-    far_recv,
     q_send,
     q_recv,
     o_send,
@@ -226,9 +225,10 @@
     def to_left(ref, recv, send=0):
         return remote(ref, ref, ring_send.at[1] if send == 0 else half_send.at[1], recv, left)
 
-    for n in range(GROUP):
-        to_right(kv.at[z, n], ring_recv.at[z, n]).start()
-        to_left(kv.at[z, n], ring_recv.at[z, n]).start()
+    pieces_of = [(n, part) for n in range(GROUP) for part in range(2)]
+    for n, part in pieces_of:
+        to_right(kv.at[z, n, part], ring_recv.at[z, n, part]).start()
+        to_left(kv.at[z, n, part], ring_recv.at[z, n, part]).start()
 
     for load in loads[7:]:
         load.start()
@@ -290,20 +290,26 @@
     def pass_on(step):
         one = slot_at(-step)
         other = slot_at(step)
-        for n in range(GROUP):
-            to_right(kv.at[one, n], ring_recv.at[one, n]).wait_recv()
-            to_right(kv.at[one, n], ring_recv.at[one, n]).start()
-            to_left(kv.at[other, n], ring_recv.at[other, n]).wait_recv()
-            to_left(kv.at[other, n], ring_recv.at[other, n]).start()
+        for n, part in pieces_of:
+            copy = to_right(kv.at[one, n, part], ring_recv.at[one, n, part])
+            copy.wait_recv()
+            copy.start()
+            copy = to_left(kv.at[other, n, part], ring_recv.at[other, n, part])
+            copy.wait_recv()
+            copy.start()
 
     def pass_on_halves(step):
         one = slot_at(-step)
         other = slot_at(step)
-        for n in range(GROUP):
-            to_right(kv.at[one, n], ring_recv.at[one, n]).wait_recv()
-            to_right(kv.at[one, n, 0], ring_recv.at[one, n], 1).start()
-            to_left(kv.at[other, n], ring_recv.at[other, n]).wait_recv()
-            to_left(kv.at[other, n, 1], far_recv.at[n], 1).start()
+        for n, part in pieces_of:
+            copy = to_right(kv.at[one, n, part], ring_recv.at[one, n, part], 1)
+            copy.wait_recv()
+            if part == 0:
+                copy.start()
+            copy = to_left(kv.at[other, n, part], ring_recv.at[other, n, part], 1)
+            copy.wait_recv()
+            if part == 1:
+                copy.start()
 
     pass_on(1)
     three = qs.at[:, pl.ds(0, LAYER - 1)]
@@ -350,8 +356,8 @@
         return shifted(r, i, LAYER)
 
     def last_step(n, carry):
-        to_right(kv.at[opposite, n, 0], ring_recv.at[opposite, n]).wait_recv()
-        to_left(kv.at[opposite, n, 1], far_recv.at[n]).wait_recv()
+        to_right(kv.at[opposite, n, 0], ring_recv.at[opposite, n, 0]).wait_recv()
+        to_left(kv.at[opposite, n, 1], ring_recv.at[opposite, n, 1]).wait_recv()
         top, total, acc = absorb(n, z, opposite)
         share = (acc / total).T.astype(BF16)
         for i in range(LAYER):
@@ -489,11 +495,11 @@
     remote(kv_stage, kv_stage, kv_send, kv_recv, peer).wait_send()
     remote(q_stage, q_stage, q_a2a_send, q_a2a_recv, peer).wait_send()
     ring_all = kv.at[pl.ds(0, far - 1)]
-    to_right(ring_all, far_recv.at[0]).wait_send()
-    to_left(ring_all, far_recv.at[0]).wait_send()
+    to_right(ring_all, ring_recv.at[0, 0, 0]).wait_send()
+    to_left(ring_all, ring_recv.at[0, 0, 0]).wait_send()
     ring_half = kv.at[0, :, 0]
-    to_right(ring_half, far_recv.at[0], 1).wait_send()
-    to_left(ring_half, far_recv.at[0], 1).wait_send()
+    to_right(ring_half, ring_recv.at[0, 0, 0], 1).wait_send()
+    to_left(ring_half, ring_recv.at[0, 0, 0], 1).wait_send()
     three = qs.at[:, pl.ds(0, LAYER - 1)]
     remote(three, three, q_send, q_recv, peer).wait_send()
     three = o_stage.at[pl.ds(0, LAYER - 1)]
@@ -506,6 +512,19 @@
     remote(halo, halo, halo_send, halo_recv, peer).wait_send()
     block_copy.wait()
     decoded_copy.wait()
+
+
+def hand_over(block_in, decoded_in, block_to, decoded_to, block, decoded, sem):
+    rooms = ((block_in, block, block_to), (decoded_in, decoded, decoded_to))
+    loads = [pltpu.make_async_copy(a, b, sem.at[i]) for i, (a, b, _) in enumerate(rooms)]
+    stores = [pltpu.make_async_copy(b, c, sem.at[2 + i]) for i, (_, b, c) in enumerate(rooms)]
+    for load in loads:
+        load.start()
+    for load, store in zip(loads, stores):
+        load.wait()
+        store.start()
+    for store in stores:
+        store.wait()
 
 
 def body(seqs, heads, *args):
@@ -603,8 +622,7 @@
             dma,
             dma((2,)),
             dma((2,)),
-            dma((layers, GROUP)),
-            dma((GROUP,)),
+            dma((layers, GROUP, 2)),
             dma,
             dma,
             dma,
@@ -623,6 +641,14 @@
             flops=1_200_000_000, bytes_accessed=5_000_000, transcendentals=1_000_000
         ),
     )(*operands)
+    block_out, decoded = pl.pallas_call(
+        hand_over,
+        out_shape=results,
+        in_specs=[anywhere] * 2,
+        out_specs=(anywhere, anywhere),
+        scratch_shapes=[pltpu.VMEM(x.shape, x.dtype) for x in results] + [dma((4,))],
+        compiler_params=pltpu.CompilerParams(vmem_limit_bytes=60 * 1024 * 1024),
+    )(block_out, decoded)
     return (
         block_out.reshape(1, TOK, 1, dim),
         decoded.reshape(1, 2, 2 * TOK, channels),

time: 69.1 us -> 67.3 us (0.974)
  local copies, waits for them, and re-layouts: 2.8 us -> 0 us
  Pallas kernels: 65.4 us -> 66.5 us
    unnamed x2 -> x0, local copies, waits for them, and re-layouts: 2.8 us -> none
    pallas_call x0 -> x1, Pallas kernels: none -> 1.46 us  [body(): pl.pallas_call(hand_over, out_shape=results, in_specs=[anywhere] * 2, out...]
where the time goes in v4:
time: 67.3 us; the launch traced here: 67.1 us
  Pallas kernels  66.5 us (99%)
    pallas_call x1, Pallas kernels, body(): pl.pallas_call(functools.partial(kernel, seqs, heads), out_shape=results,...  65 us
    pallas_call x1, Pallas kernels, body(): pl.pallas_call(hand_over, out_shape=results, in_specs=[anywhere] * 2, out...  1.46 us

profile of v4, /device:TPU:1, one launch (start us, length us, event | category | flops | bytes accessed | tf_op | source)
XLA Modules:
  0.0 67.1 jit_solution(13418045115914603783)
XLA Ops:
  0.6 65.0 %shard_map.167 = (bf16[8,3072]{1,0:T(8,128)(2,1)}, bf16[2,16,512]{2,1,0:T(8,128)(2,1)}) custom-call(bf16[8,3072]{1,0:T(8,128)(2,1)} %bitcast.17, bf16[8,3072]{1,0:T(8,128)(2,1)} %bitcast.18, bf16[8,3072]{1,0:T(8,128)(2,1)} %bitcast.19, bf16[256,384]{1,0:T(8,128)(2,1)} %text_k_hbm.1, bf16[256,384]{1,0:T(8,128)(2,1)} %text_v_hbm.1, s32[1,256]{1,0:T(1,128)} %bitcast.28, ...), custom_call_target="tpu_custom_call" | custom-call | flops 1200000000 | bytes 5000000 | tf_op jit(solution)/shard_map/pallas_call | solution.py:584
  65.6 1.5 %shard_map.168 = (bf16[8,3072]{1,0:T(8,128)(2,1)}, bf16[2,16,512]{2,1,0:T(8,128)(2,1)}) custom-call(bf16[8,3072]{1,0:T(8,128)(2,1)} %get-tuple-element.6.block_in, bf16[2,16,512]{2,1,0:T(8,128)(2,1)} %get-tuple-element.7.decoded_in), custom_call_target="tpu_custom_call" | custom-call | tf_op jit(solution)/shard_map/pallas_call | solution.py:644

commit v5 on v4

--- a/solution.py
+++ b/solution.py
@@ -207,6 +207,28 @@
     for load in loads[3:7]:
         load.start()
 
+    taps = w_sum.shape[0]
+    parities = w_full.shape[0]
+    features = final_w.shape[0]
+
+    def sum_taps():
+        conv_all = conv_w[...].astype(F32)
+        total = conv_all[:taps] + conv_all[taps : 2 * taps] + conv_all[2 * taps :]
+        w_sum[...] = total.astype(BF16)
+
+    def conv_weights(parity):
+        up = parity // 2
+        side = lax.rem(parity, 2)
+        depth = w_full.shape[1]
+        row = lax.broadcasted_iota(jnp.int32, (depth, taps), 0)
+        col = lax.broadcasted_iota(jnp.int32, (depth, taps), 1)
+        tap_i = 2 * (row >> 7) + ((row >> 1) & 1) + up - 1
+        tap_j = 2 * ((row >> 6) & 1) + (row & 1) + side - 1
+        inside = (tap_i >= 0) & (tap_i <= 2) & (tap_j >= 0) & (tap_j <= 2)
+        source = (tap_i * 3 + tap_j) * LAT_CH + ((row & 63) >> 2)
+        pick = jnp.where(inside & (source == col), 1.0, 0.0).astype(BF16)
+        w_full[parity] = dot(pick, w_sum[...]).astype(BF16)
+
     def rows_of(block):
         return block.astype(F32).reshape(rows, width).astype(BF16)
 
@@ -226,12 +248,16 @@
         return remote(ref, ref, ring_send.at[1] if send == 0 else half_send.at[1], recv, left)
 
     pieces_of = [(n, part) for n in range(GROUP) for part in range(2)]
-    for n, part in pieces_of:
+
+    def first_piece(at):
+        n, part = pieces_of[at]
         to_right(kv.at[z, n, part], ring_recv.at[z, n, part]).start()
         to_left(kv.at[z, n, part], ring_recv.at[z, n, part]).start()
 
+    first_piece(0)
     for load in loads[7:]:
         load.start()
+    first_piece(1)
 
     remote(q_in, q_in, q_a2a_send, q_a2a_recv, peer).wait_recv()
     own_q = rows_of(q_in[...])
@@ -239,6 +265,15 @@
         qs[n, r] = own_q[:, n * HEAD_DIM : (n + 1) * HEAD_DIM]
     for i in range(1, LAYER):
         remote(qs.at[:, r], qs.at[:, r], q_send, q_recv, layer_peer(i)).start()
+    first_piece(2)
+    loads[3].wait()
+    sum_taps()
+    first_piece(3)
+    conv_weights(jnp.int32(0))
+    first_piece(4)
+    conv_weights(jnp.int32(1))
+    first_piece(5)
+    made = 2
 
     def attend_text(n):
         share = text_k.shape[0] // LAYER
@@ -265,32 +300,10 @@
         acc = run_acc[n] * factor + dot_tn(values_now, weights.astype(BF16))
         return top, total, acc
 
-    taps = w_sum.shape[0]
-    parities = w_full.shape[0]
-    features = final_w.shape[0]
-
-    def sum_taps():
-        conv_all = conv_w[...].astype(F32)
-        total = conv_all[:taps] + conv_all[taps : 2 * taps] + conv_all[2 * taps :]
-        w_sum[...] = total.astype(BF16)
-
-    def conv_weights(parity):
-        up = parity // 2
-        side = lax.rem(parity, 2)
-        depth = w_full.shape[1]
-        row = lax.broadcasted_iota(jnp.int32, (depth, taps), 0)
-        col = lax.broadcasted_iota(jnp.int32, (depth, taps), 1)
-        tap_i = 2 * (row >> 7) + ((row >> 1) & 1) + up - 1
-        tap_j = 2 * ((row >> 6) & 1) + (row & 1) + side - 1
-        inside = (tap_i >= 0) & (tap_i <= 2) & (tap_j >= 0) & (tap_j <= 2)
-        source = (tap_i * 3 + tap_j) * LAT_CH + ((row & 63) >> 2)
-        pick = jnp.where(inside & (source == col), 1.0, 0.0).astype(BF16)
-        w_full[parity] = dot(pick, w_sum[...]).astype(BF16)
-
-    def pass_on(step):
+    def pass_on(step, n):
         one = slot_at(-step)
         other = slot_at(step)
-        for n, part in pieces_of:
+        for part in range(2):
             copy = to_right(kv.at[one, n, part], ring_recv.at[one, n, part])
             copy.wait_recv()
             copy.start()
@@ -298,10 +311,10 @@
             copy.wait_recv()
             copy.start()
 
-    def pass_on_halves(step):
+    def pass_on_halves(step, n):
         one = slot_at(-step)
         other = slot_at(step)
-        for n, part in pieces_of:
+        for part in range(2):
             copy = to_right(kv.at[one, n, part], ring_recv.at[one, n, part], 1)
             copy.wait_recv()
             if part == 0:
@@ -311,42 +324,44 @@
             if part == 1:
                 copy.start()
 
-    pass_on(1)
+    pass_on(1, 0)
     three = qs.at[:, pl.ds(0, LAYER - 1)]
     remote(three, three, q_send, q_recv, layer_peer(1)).wait_recv()
     for n in range(GROUP):
         q_turned[n] = qs[n].reshape(LAYER * rows, HEAD_DIM).T
-    for load in loads[3:7]:
+    pass_on(1, 1)
+    for load in loads[4:7]:
         load.wait()
     mask_column[...] = jnp.broadcast_to(mask[...].astype(F32), (TOK, mask.shape[1])).T
-    for n in range(GROUP):
+    attend_text(0)
+    pass_on(1, 2)
+    for n in range(1, GROUP):
         attend_text(n)
-    sum_taps()
-    in_loop = min(parities, max(0, far - 3))
+    in_loop = min(parities - made, max(0, far - 3))
 
     def ring_step(step, carry):
-        @pl.when(step < far - 1)
-        def _():
-            pass_on(step)
-
-        @pl.when(step == far - 1)
-        def _():
-            pass_on_halves(step)
-
-        news = [absorb(n, slot_at(1 - step), slot_at(step - 1)) for n in range(GROUP)]
-        for n, (top, total, acc) in enumerate(news):
+        for n in range(GROUP):
+            @pl.when(step < far - 1)
+            def _():
+                pass_on(step, n)
+
+            @pl.when(step == far - 1)
+            def _():
+                pass_on_halves(step, n)
+
+            top, total, acc = absorb(n, slot_at(1 - step), slot_at(step - 1))
             run_max[n, :1] = top
             run_sum[n, :1] = total
             run_acc[n] = acc
 
         @pl.when(step - 2 < in_loop)
         def _():
-            conv_weights(step - 2)
+            conv_weights(step - 2 + made)
 
         return carry
 
     lax.fori_loop(2, far + 1, ring_step, 0)
-    for parity in range(in_loop, parities):
+    for parity in range(made + in_loop, parities):
         conv_weights(jnp.int32(parity))
 
     opposite = slot_at(far)

time: 67.3 us -> 68.1 us (1.012)
  Pallas kernels: 66.5 us -> 67.3 us
    pallas_call x1, Pallas kernels: 65 us -> 65.8 us  [body(): pl.pallas_call(functools.partial(kernel, seqs, heads), out_shape=results,...]
where the time goes in v5:
time: 68.1 us; the launch traced here: 67.9 us
  Pallas kernels  67.3 us (99%)
    pallas_call x1, Pallas kernels, body(): pl.pallas_call(functools.partial(kernel, seqs, heads), out_shape=results,...  65.8 us
    pallas_call x1, Pallas kernels, body(): pl.pallas_call(hand_over, out_shape=results, in_specs=[anywhere] * 2, out...  1.46 us

profile of v5, /device:TPU:1, one launch (start us, length us, event | category | flops | bytes accessed | tf_op | source)
XLA Modules:
  0.0 67.9 jit_solution(7750356951099599294)
XLA Ops:
  0.6 65.8 %shard_map.167 = (bf16[8,3072]{1,0:T(8,128)(2,1)}, bf16[2,16,512]{2,1,0:T(8,128)(2,1)}) custom-call(bf16[8,3072]{1,0:T(8,128)(2,1)} %bitcast.17, bf16[8,3072]{1,0:T(8,128)(2,1)} %bitcast.18, bf16[8,3072]{1,0:T(8,128)(2,1)} %bitcast.19, bf16[256,384]{1,0:T(8,128)(2,1)} %text_k_hbm.1, bf16[256,384]{1,0:T(8,128)(2,1)} %text_v_hbm.1, s32[1,256]{1,0:T(1,128)} %bitcast.28, ...), custom_call_target="tpu_custom_call" | custom-call | flops 1200000000 | bytes 5000000 | tf_op jit(solution)/shard_map/pallas_call | solution.py:599
  66.4 1.5 %shard_map.168 = (bf16[8,3072]{1,0:T(8,128)(2,1)}, bf16[2,16,512]{2,1,0:T(8,128)(2,1)}) custom-call(bf16[8,3072]{1,0:T(8,128)(2,1)} %get-tuple-element.6.block_in, bf16[2,16,512]{2,1,0:T(8,128)(2,1)} %get-tuple-element.7.decoded_in), custom_call_target="tpu_custom_call" | custom-call | tf_op jit(solution)/shard_map/pallas_call | solution.py:659

commit v6 on v5

--- a/solution.py
+++ b/solution.py
@@ -12,6 +12,7 @@
 LAT_CH = 16
 TOK = 8
 LAYER = 4
+STRIDE = 3
 LATENT_SCALE = 0.476986
 NEG = -1e30
 SCORE_SCALE = HEAD_DIM ** (-0.5)
@@ -104,6 +105,7 @@
     q_a2a_recv,
     ring_send,
     half_send,
+    long_send,
     ring_recv,
     q_send,
     q_recv,
@@ -142,8 +144,11 @@
     def slot_at(by):
         return lax.rem(z + by + layers, layers)
 
-    right = (slot_at(1) * LAYER + j, h)
-    left = (slot_at(-1) * LAYER + j, h)
+    def ring_peer(by):
+        return (slot_at(by) * LAYER + j, h)
+
+    right, left = ring_peer(1), ring_peer(-1)
+    far_right, far_left = ring_peer(STRIDE), ring_peer(-STRIDE)
 
     def remote(src, dst, send, recv, device):
         return pltpu.make_async_remote_copy(
@@ -181,7 +186,7 @@
     halo_peers = [(shifted(s, dr, seqs), shifted(h, dc, heads)) for dr, dc in halo_steps]
     partners = [head_peer(i) for i in range(heads)]
     partners += [layer_peer(i) for i in range(1, LAYER)]
-    partners += [right, left]
+    partners += [right, left, far_right, far_left]
     partners += halo_peers
     for load in loads[:3]:
         load.start()
@@ -195,15 +200,21 @@
             kv_stage[g, at] = whole[:, cols]
     pl.semaphore_wait(barrier, len(partners))
 
-    for i in range(heads):
-        peer = head_peer(i)
-        remote(kv_stage.at[peer[1]], kv_in.at[h], kv_send, kv_recv, peer).start()
+    def send_kv(i, carry):
+        to = head_peer(i)
+        remote(kv_stage.at[to[1]], kv_in.at[h], kv_send, kv_recv, to).start()
+        return carry
+
+    def send_q(i, carry):
+        to = head_peer(i)
+        remote(q_stage.at[to[1]], q_in.at[h], q_a2a_send, q_a2a_recv, to).start()
+        return carry
+
+    lax.fori_loop(0, heads, send_kv, 0)
     loads[2].wait()
     for g, cols in enumerate(group_cols):
         q_stage[g] = queries[:, cols]
-    for i in range(heads):
-        peer = head_peer(i)
-        remote(q_stage.at[peer[1]], q_in.at[h], q_a2a_send, q_a2a_recv, peer).start()
+    lax.fori_loop(0, heads, send_q, 0)
     for load in loads[3:7]:
         load.start()
 
@@ -249,15 +260,15 @@
 
     pieces_of = [(n, part) for n in range(GROUP) for part in range(2)]
 
-    def first_piece(at):
-        n, part = pieces_of[at]
+    for n, part in pieces_of:
+        ref, recv = kv.at[z, n, part], ring_recv.at[z, n, part]
+        remote(ref, ref, long_send.at[0], recv, far_right).start()
+        remote(ref, ref, long_send.at[1], recv, far_left).start()
+    for n, part in pieces_of:
         to_right(kv.at[z, n, part], ring_recv.at[z, n, part]).start()
         to_left(kv.at[z, n, part], ring_recv.at[z, n, part]).start()
-
-    first_piece(0)
     for load in loads[7:]:
         load.start()
-    first_piece(1)
 
     remote(q_in, q_in, q_a2a_send, q_a2a_recv, peer).wait_recv()
     own_q = rows_of(q_in[...])
@@ -265,20 +276,15 @@
         qs[n, r] = own_q[:, n * HEAD_DIM : (n + 1) * HEAD_DIM]
     for i in range(1, LAYER):
         remote(qs.at[:, r], qs.at[:, r], q_send, q_recv, layer_peer(i)).start()
-    first_piece(2)
     loads[3].wait()
     sum_taps()
-    first_piece(3)
     conv_weights(jnp.int32(0))
-    first_piece(4)
-    conv_weights(jnp.int32(1))
-    first_piece(5)
-    made = 2
+    made = 1
 
     def attend_text(n):
         share = text_k.shape[0] // LAYER
         mine = pl.ds(pl.multiple_of(j * share, share), share)
-        cols = slice(n * HEAD_DIM, (n + 1) * HEAD_DIM)
+        cols = pl.ds(pl.multiple_of(n * HEAD_DIM, HEAD_DIM), HEAD_DIM)
         scores = dot(text_k[mine, cols], q_turned[n])
         real = jnp.broadcast_to(mask_column[mine, :1] == 1.0, scores.shape)
         scores = jnp.where(real, scores, NEG)
@@ -324,23 +330,52 @@
             if part == 1:
                 copy.start()
 
-    pass_on(1, 0)
+    def keep(step, n):
+        one = slot_at(-step)
+        other = slot_at(step)
+        for part in range(2):
+            to_right(kv.at[one, n, part], ring_recv.at[one, n, part]).wait_recv()
+            to_left(kv.at[other, n, part], ring_recv.at[other, n, part]).wait_recv()
+
+    def work_on(step, n):
+        top, total, acc = absorb(n, slot_at(-step), slot_at(step))
+        run_max[n, :1] = top
+        run_sum[n, :1] = total
+        run_acc[n] = acc
+
+    def each_head(take, taken, worked):
+        def one_head(n, carry):
+            if take is not None:
+                take(taken, n)
+            if worked is not None:
+                work_on(worked, n)
+            return carry
+
+        lax.fori_loop(0, GROUP, one_head, 0)
+
+    each_head(pass_on, STRIDE, None)
+    each_head(pass_on, 1, None)
     three = qs.at[:, pl.ds(0, LAYER - 1)]
     remote(three, three, q_send, q_recv, layer_peer(1)).wait_recv()
     for n in range(GROUP):
         q_turned[n] = qs[n].reshape(LAYER * rows, HEAD_DIM).T
-    pass_on(1, 1)
     for load in loads[4:7]:
         load.wait()
     mask_column[...] = jnp.broadcast_to(mask[...].astype(F32), (TOK, mask.shape[1])).T
-    attend_text(0)
-    pass_on(1, 2)
-    for n in range(1, GROUP):
+
+    def text_head(n, carry):
         attend_text(n)
-    in_loop = min(parities - made, max(0, far - 3))
+        return carry
+
+    lax.fori_loop(0, GROUP, text_head, 0)
+    each_head(pass_on if far > 5 else pass_on_halves, 4, STRIDE)
+    conv_weights(jnp.int32(1))
+    made = 2
+    each_head(keep, 2, 1)
+    in_loop = min(parities - made, max(0, far - 5))
 
     def ring_step(step, carry):
-        for n in range(GROUP):
+        def one_head(n, inner):
             @pl.when(step < far - 1)
             def _():
                 pass_on(step, n)
@@ -349,20 +384,27 @@
             def _():
                 pass_on_halves(step, n)
 
-            top, total, acc = absorb(n, slot_at(1 - step), slot_at(step - 1))
-            run_max[n, :1] = top
-            run_sum[n, :1] = total
-            run_acc[n] = acc
-
-        @pl.when(step - 2 < in_loop)
+            work_on(step - 1, n)
+            return inner
+
+        lax.fori_loop(0, GROUP, one_head, 0)
+
+        @pl.when(step - 5 < in_loop)
         def _():
-            conv_weights(step - 2 + made)
+            conv_weights(step - 5 + made)
 
         return carry
 
-    lax.fori_loop(2, far + 1, ring_step, 0)
+    if far > 5:
+        lax.fori_loop(5, far, ring_step, 0)
     for parity in range(made + in_loop, parities):
         conv_weights(jnp.int32(parity))
+
+    def last_two(i, carry):
+        each_head(None, 0, 2 + i * (far - 3))
+        return carry
+
+    lax.fori_loop(0, 2, last_two, 0)
 
     opposite = slot_at(far)
     marks[...] = jnp.zeros_like(marks)
@@ -436,7 +478,8 @@
     for part in range(rs_parts):
         product = dot(attended, out_w[:, part * part_cols : (part + 1) * part_cols])
         rs_stage[part] = product.reshape(heads, TOK, part_cols).astype(BF16)
-        for i in range(heads):
+
+        def send_part(i, carry, part=part):
             to = head_peer(i)
             remote(
                 rs_stage.at[part, to[1]],
@@ -445,6 +488,9 @@
                 rs_recv.at[part],
                 to,
             ).start()
+            return carry
+
+        lax.fori_loop(0, heads, send_part, 0)
     pieces = []
     for part in range(rs_parts):
         cols = slice(part * part_cols, (part + 1) * part_cols)
@@ -509,7 +555,10 @@
 
     remote(kv_stage, kv_stage, kv_send, kv_recv, peer).wait_send()
     remote(q_stage, q_stage, q_a2a_send, q_a2a_recv, peer).wait_send()
-    ring_all = kv.at[pl.ds(0, far - 1)]
+    ring_one = kv.at[0]
+    remote(ring_one, ring_one, long_send.at[0], ring_recv.at[0, 0, 0], far_right).wait_send()
+    remote(ring_one, ring_one, long_send.at[1], ring_recv.at[0, 0, 0], far_left).wait_send()
+    ring_all = kv.at[pl.ds(0, far - 2)]
     to_right(ring_all, ring_recv.at[0, 0, 0]).wait_send()
     to_left(ring_all, ring_recv.at[0, 0, 0]).wait_send()
     ring_half = kv.at[0, :, 0]
@@ -637,6 +686,7 @@
             dma,
             dma((2,)),
             dma((2,)),
+            dma((2,)),
             dma((layers, GROUP, 2)),
             dma,
             dma,

time: 68.1 us -> 67.7 us (level)
  no operation moved by 1% of the time
where the time goes in v6:
time: 67.7 us; the launch traced here: 67.5 us
  Pallas kernels  66.9 us (99%)
    pallas_call x1, Pallas kernels, body(): pl.pallas_call(functools.partial(kernel, seqs, heads), out_shape=results,...  65.4 us
    pallas_call x1, Pallas kernels, body(): pl.pallas_call(hand_over, out_shape=results, in_specs=[anywhere] * 2, out...  1.46 us

profile of v6, /device:TPU:1, one launch (start us, length us, event | category | flops | bytes accessed | tf_op | source)
XLA Modules:
  0.0 67.5 jit_solution(936809003186652393)
XLA Ops:
  0.6 65.4 %shard_map.167 = (bf16[8,3072]{1,0:T(8,128)(2,1)}, bf16[2,16,512]{2,1,0:T(8,128)(2,1)}) custom-call(bf16[8,3072]{1,0:T(8,128)(2,1)} %bitcast.17, bf16[8,3072]{1,0:T(8,128)(2,1)} %bitcast.18, bf16[8,3072]{1,0:T(8,128)(2,1)} %bitcast.19, bf16[256,384]{1,0:T(8,128)(2,1)} %text_k_hbm.1, bf16[256,384]{1,0:T(8,128)(2,1)} %text_v_hbm.1, s32[1,256]{1,0:T(1,128)} %bitcast.28, ...), custom_call_target="tpu_custom_call" | custom-call | flops 1200000000 | bytes 5000000 | tf_op jit(solution)/shard_map/pallas_call | solution.py:648
  66.0 1.5 %shard_map.168 = (bf16[8,3072]{1,0:T(8,128)(2,1)}, bf16[2,16,512]{2,1,0:T(8,128)(2,1)}) custom-call(bf16[8,3072]{1,0:T(8,128)(2,1)} %get-tuple-element.6.block_in, bf16[2,16,512]{2,1,0:T(8,128)(2,1)} %get-tuple-element.7.decoded_in), custom_call_target="tpu_custom_call" | custom-call | tf_op jit(solution)/shard_map/pallas_call | solution.py:709

commit v7 on v5

--- a/solution.py
+++ b/solution.py
@@ -142,8 +142,10 @@
     def slot_at(by):
         return lax.rem(z + by + layers, layers)
 
-    right = (slot_at(1) * LAYER + j, h)
-    left = (slot_at(-1) * LAYER + j, h)
+    def ring_peer(by):
+        return (slot_at(by) * LAYER + j, h)
+
+    right, left = ring_peer(1), ring_peer(-1)
 
     def remote(src, dst, send, recv, device):
         return pltpu.make_async_remote_copy(
@@ -195,15 +197,21 @@
             kv_stage[g, at] = whole[:, cols]
     pl.semaphore_wait(barrier, len(partners))
 
-    for i in range(heads):
-        peer = head_peer(i)
-        remote(kv_stage.at[peer[1]], kv_in.at[h], kv_send, kv_recv, peer).start()
+    def send_kv(i, carry):
+        to = head_peer(i)
+        remote(kv_stage.at[to[1]], kv_in.at[h], kv_send, kv_recv, to).start()
+        return carry
+
+    def send_q(i, carry):
+        to = head_peer(i)
+        remote(q_stage.at[to[1]], q_in.at[h], q_a2a_send, q_a2a_recv, to).start()
+        return carry
+
+    lax.fori_loop(0, heads, send_kv, 0)
     loads[2].wait()
     for g, cols in enumerate(group_cols):
         q_stage[g] = queries[:, cols]
-    for i in range(heads):
-        peer = head_peer(i)
-        remote(q_stage.at[peer[1]], q_in.at[h], q_a2a_send, q_a2a_recv, peer).start()
+    lax.fori_loop(0, heads, send_q, 0)
     for load in loads[3:7]:
         load.start()
 
@@ -249,15 +257,11 @@
 
     pieces_of = [(n, part) for n in range(GROUP) for part in range(2)]
 
-    def first_piece(at):
-        n, part = pieces_of[at]
+    for n, part in pieces_of:
         to_right(kv.at[z, n, part], ring_recv.at[z, n, part]).start()
         to_left(kv.at[z, n, part], ring_recv.at[z, n, part]).start()
-
-    first_piece(0)
     for load in loads[7:]:
         load.start()
-    first_piece(1)
 
     remote(q_in, q_in, q_a2a_send, q_a2a_recv, peer).wait_recv()
     own_q = rows_of(q_in[...])
@@ -265,104 +269,117 @@
         qs[n, r] = own_q[:, n * HEAD_DIM : (n + 1) * HEAD_DIM]
     for i in range(1, LAYER):
         remote(qs.at[:, r], qs.at[:, r], q_send, q_recv, layer_peer(i)).start()
-    first_piece(2)
-    loads[3].wait()
-    sum_taps()
-    first_piece(3)
-    conv_weights(jnp.int32(0))
-    first_piece(4)
-    conv_weights(jnp.int32(1))
-    first_piece(5)
-    made = 2
-
-    def attend_text(n):
+    def weigh(scores, top):
+        return jnp.exp2((scores - top) * (SCORE_SCALE * LOG2E))
+
+    def attend_first(n, carry):
         share = text_k.shape[0] // LAYER
         mine = pl.ds(pl.multiple_of(j * share, share), share)
-        cols = slice(n * HEAD_DIM, (n + 1) * HEAD_DIM)
-        scores = dot(text_k[mine, cols], q_turned[n])
-        real = jnp.broadcast_to(mask_column[mine, :1] == 1.0, scores.shape)
+        cols = pl.ds(pl.multiple_of(n * HEAD_DIM, HEAD_DIM), HEAD_DIM)
+        keys_now = jnp.concatenate([text_k[mine, cols], kv[z, n, 0]], axis=0)
+        values_now = jnp.concatenate([text_v[mine, cols], kv[z, n, 1]], axis=0)
+        scores = dot(keys_now, q_turned[n])
+        real = jnp.concatenate([mask_column[mine, :1], jnp.ones((rows, 1), F32)], axis=0) == 1.0
+        real = jnp.broadcast_to(real, scores.shape)
         scores = jnp.where(real, scores, NEG)
         top = jnp.max(scores, axis=0, keepdims=True)
-        weights = jnp.where(real, jnp.exp2((scores - top) * (SCORE_SCALE * LOG2E)), 0.0)
+        weights = jnp.where(real, weigh(scores, top), 0.0)
         run_max[n, :1] = top
         run_sum[n, :1] = jnp.sum(weights, axis=0, keepdims=True)
-        run_acc[n] = dot_tn(text_v[mine, cols], weights.astype(BF16))
-
-    def absorb(n, one, other):
-        keys_now = jnp.concatenate([kv[one, n, 0], kv[other, n, 0]], axis=0)
-        values_now = jnp.concatenate([kv[one, n, 1], kv[other, n, 1]], axis=0)
+        run_acc[n] = dot_tn(values_now, weights.astype(BF16))
+        return carry
+
+    def absorb(n, slots):
+        keys_now = jnp.concatenate([kv[slot, n, 0] for slot in slots], axis=0)
+        values_now = jnp.concatenate([kv[slot, n, 1] for slot in slots], axis=0)
         scores = dot(keys_now, q_turned[n])
         old = run_max[n, :1]
         top = jnp.maximum(old, jnp.max(scores, axis=0, keepdims=True))
-        factor = jnp.exp2((old - top) * (SCORE_SCALE * LOG2E))
-        weights = jnp.exp2((scores - top) * (SCORE_SCALE * LOG2E))
+        factor = weigh(old, top)
+        weights = weigh(scores, top)
         total = run_sum[n, :1] * factor + jnp.sum(weights, axis=0, keepdims=True)
         acc = run_acc[n] * factor + dot_tn(values_now, weights.astype(BF16))
         return top, total, acc
 
-    def pass_on(step, n):
+    def work_on(n, steps):
+        top, total, acc = absorb(n, [slot_at(by) for step in steps for by in (-step, step)])
+        run_max[n, :1] = top
+        run_sum[n, :1] = total
+        run_acc[n] = acc
+
+    def pass_on(step):
         one = slot_at(-step)
         other = slot_at(step)
-        for part in range(2):
-            copy = to_right(kv.at[one, n, part], ring_recv.at[one, n, part])
-            copy.wait_recv()
-            copy.start()
-            copy = to_left(kv.at[other, n, part], ring_recv.at[other, n, part])
-            copy.wait_recv()
-            copy.start()
-
-    def pass_on_halves(step, n):
+
+        def one_head(n, carry):
+            for part in range(2):
+                copy = to_right(kv.at[one, n, part], ring_recv.at[one, n, part])
+                copy.wait_recv()
+                copy.start()
+                copy = to_left(kv.at[other, n, part], ring_recv.at[other, n, part])
+                copy.wait_recv()
+                copy.start()
+            return carry
+
+        lax.fori_loop(0, GROUP, one_head, 0)
+
+    def pass_on_halves(step):
         one = slot_at(-step)
         other = slot_at(step)
-        for part in range(2):
-            copy = to_right(kv.at[one, n, part], ring_recv.at[one, n, part], 1)
-            copy.wait_recv()
-            if part == 0:
-                copy.start()
-            copy = to_left(kv.at[other, n, part], ring_recv.at[other, n, part], 1)
-            copy.wait_recv()
-            if part == 1:
-                copy.start()
-
-    pass_on(1, 0)
+
+        def one_head(n, carry):
+            for part in range(2):
+                copy = to_right(kv.at[one, n, part], ring_recv.at[one, n, part], 1)
+                copy.wait_recv()
+                if part == 0:
+                    copy.start()
+                copy = to_left(kv.at[other, n, part], ring_recv.at[other, n, part], 1)
+                copy.wait_recv()
+                if part == 1:
+                    copy.start()
+            return carry
+
+        lax.fori_loop(0, GROUP, one_head, 0)
+
+    pass_on(1)
     three = qs.at[:, pl.ds(0, LAYER - 1)]
     remote(three, three, q_send, q_recv, layer_peer(1)).wait_recv()
     for n in range(GROUP):
         q_turned[n] = qs[n].reshape(LAYER * rows, HEAD_DIM).T
-    pass_on(1, 1)
-    for load in loads[4:7]:
+    for load in loads[3:7]:
         load.wait()
     mask_column[...] = jnp.broadcast_to(mask[...].astype(F32), (TOK, mask.shape[1])).T
-    attend_text(0)
-    pass_on(1, 2)
-    for n in range(1, GROUP):
-        attend_text(n)
-    in_loop = min(parities - made, max(0, far - 3))
-
-    def ring_step(step, carry):
-        for n in range(GROUP):
-            @pl.when(step < far - 1)
-            def _():
-                pass_on(step, n)
-
-            @pl.when(step == far - 1)
-            def _():
-                pass_on_halves(step, n)
-
-            top, total, acc = absorb(n, slot_at(1 - step), slot_at(step - 1))
-            run_max[n, :1] = top
-            run_sum[n, :1] = total
-            run_acc[n] = acc
-
-        @pl.when(step - 2 < in_loop)
+    lax.fori_loop(0, GROUP, attend_first, 0)
+    pass_on(2)
+    sum_taps()
+
+    def two_parities(first):
+        def one_parity(parity, carry):
+            conv_weights(parity)
+            return carry
+
+        lax.fori_loop(first, first + 2, one_parity, 0)
+
+    two_parities(0)
+    pass_on(3)
+    two_parities(2)
+
+    def middle_step(n, carry):
+        @pl.when(n + 4 < far - 1)
         def _():
-            conv_weights(step - 2 + made)
-
+            pass_on(n + 4)
+
+        work_on(n, range(1, far - 4))
         return carry
 
-    lax.fori_loop(2, far + 1, ring_step, 0)
-    for parity in range(made + in_loop, parities):
-        conv_weights(jnp.int32(parity))
+    lax.fori_loop(0, GROUP, middle_step, 0)
+    pass_on_halves(far - 1)
+
+    def late_step(n, carry):
+        work_on(n, range(far - 4, far - 1))
+        return carry
+
+    lax.fori_loop(0, GROUP, late_step, 0)
 
     opposite = slot_at(far)
     marks[...] = jnp.zeros_like(marks)
@@ -373,7 +390,7 @@
     def last_step(n, carry):
         to_right(kv.at[opposite, n, 0], ring_recv.at[opposite, n, 0]).wait_recv()
         to_left(kv.at[opposite, n, 1], ring_recv.at[opposite, n, 1]).wait_recv()
-        top, total, acc = absorb(n, z, opposite)
+        top, total, acc = absorb(n, [slot_at(1 - far), slot_at(far - 1), opposite])
         share = (acc / total).T.astype(BF16)
         for i in range(LAYER):
             o_stage[i, n] = share[i * rows : (i + 1) * rows]
@@ -436,7 +453,8 @@
     for part in range(rs_parts):
         product = dot(attended, out_w[:, part * part_cols : (part + 1) * part_cols])
         rs_stage[part] = product.reshape(heads, TOK, part_cols).astype(BF16)
-        for i in range(heads):
+
+        def send_part(i, carry, part=part):
             to = head_peer(i)
             remote(
                 rs_stage.at[part, to[1]],
@@ -445,6 +463,9 @@
                 rs_recv.at[part],
                 to,
             ).start()
+            return carry
+
+        lax.fori_loop(0, heads, send_part, 0)
     pieces = []
     for part in range(rs_parts):
         cols = slice(part * part_cols, (part + 1) * part_cols)

time: 68.1 us -> 67.4 us (0.990)
  Pallas kernels: 67.3 us -> 66.5 us
    pallas_call x1, Pallas kernels: 65.8 us -> 65 us  [body(): pl.pallas_call(functools.partial(kernel, seqs, heads), out_shape=results,...]
where the time goes in v7:
time: 67.4 us; the launch traced here: 67.2 us
  Pallas kernels  66.5 us (99%)
    pallas_call x1, Pallas kernels, body(): pl.pallas_call(functools.partial(kernel, seqs, heads), out_shape=results,...  65 us
    pallas_call x1, Pallas kernels, body(): pl.pallas_call(hand_over, out_shape=results, in_specs=[anywhere] * 2, out...  1.46 us

profile of v7, /device:TPU:1, one launch (start us, length us, event | category | flops | bytes accessed | tf_op | source)
XLA Modules:
  0.0 67.2 jit_solution(17107081937781705965)
XLA Ops:
  0.6 65.0 %shard_map.167 = (bf16[8,3072]{1,0:T(8,128)(2,1)}, bf16[2,16,512]{2,1,0:T(8,128)(2,1)}) custom-call(bf16[8,3072]{1,0:T(8,128)(2,1)} %bitcast.17, bf16[8,3072]{1,0:T(8,128)(2,1)} %bitcast.18, bf16[8,3072]{1,0:T(8,128)(2,1)} %bitcast.19, bf16[256,384]{1,0:T(8,128)(2,1)} %text_k_hbm.1, bf16[256,384]{1,0:T(8,128)(2,1)} %text_v_hbm.1, s32[1,256]{1,0:T(1,128)} %bitcast.28, ...), custom_call_target="tpu_custom_call" | custom-call | flops 1200000000 | bytes 5000000 | tf_op jit(solution)/shard_map/pallas_call | solution.py:620
  65.7 1.5 %shard_map.168 = (bf16[8,3072]{1,0:T(8,128)(2,1)}, bf16[2,16,512]{2,1,0:T(8,128)(2,1)}) custom-call(bf16[8,3072]{1,0:T(8,128)(2,1)} %get-tuple-element.6.block_in, bf16[2,16,512]{2,1,0:T(8,128)(2,1)} %get-tuple-element.7.decoded_in), custom_call_target="tpu_custom_call" | custom-call | tf_op jit(solution)/shard_map/pallas_call | solution.py:680

commit v8 on v7

--- a/solution.py
+++ b/solution.py
@@ -12,6 +12,8 @@
 LAT_CH = 16
 TOK = 8
 LAYER = 4
+PAIR = 8
+COLUMNS = 4
 LATENT_SCALE = 0.476986
 NEG = -1e30
 SCORE_SCALE = HEAD_DIM ** (-0.5)
@@ -118,10 +120,17 @@
 ):
     s = lax.axis_index("seq")
     h = lax.axis_index("head")
-    layers = seqs // LAYER
+    layers = seqs // PAIR
     far = layers // 2
-    z = s // LAYER
+    depth = s // LAYER
     j = lax.rem(s, LAYER)
+    z = depth // 2
+    parity_z = lax.rem(depth, 2)
+    column = lax.rem(h, COLUMNS)
+    y_high = h // COLUMNS
+    part_of = y_high * LAYER + j
+    place = parity_z * COLUMNS + column
+    apart = lax.rem(y_high + parity_z, 2)
     width = GROUP * HEAD_DIM
     dim = heads * width
     rows = heads * TOK
@@ -134,16 +143,37 @@
     r = lax.rem(j + LAYER // 2, LAYER)
 
     def head_peer(i):
-        return (z * LAYER + r, shifted(h, i, heads))
-
-    def layer_peer(i):
-        return (z * LAYER + shifted(j, i, LAYER), h)
+        return (depth * LAYER + r, shifted(h, i, heads))
+
+    def group_peer(i):
+        at_depth = z * 2 + lax.rem(parity_z + i // COLUMNS, 2)
+        at_column = lax.rem(column + lax.rem(i, COLUMNS), COLUMNS)
+        group = lax.rem(at_depth, 2) * COLUMNS + at_column
+        return (at_depth * LAYER + j, y_high * COLUMNS + at_column), group
+
+    def part_peer(i):
+        part = lax.rem(part_of + i, PAIR)
+        return (depth * LAYER + lax.rem(part, LAYER), (part // LAYER) * COLUMNS + column)
+
+    def row_peer(i):
+        at_parity = lax.rem(parity_z + i // LAYER, 2)
+        row = lax.rem(j + lax.rem(i, LAYER), LAYER)
+        owner = lax.rem(row + LAYER // 2, LAYER)
+        to = ((z * 2 + at_parity) * LAYER + owner, parity_z * COLUMNS + column)
+        return to, at_parity * LAYER + row
+
+    own_row = LAYER // 2
+
+    def share_source(i):
+        part = lax.rem(part_of + i, PAIR)
+        at = (z * 2 + y_high) * LAYER + lax.rem(part, LAYER)
+        return (at, (part // LAYER) * COLUMNS + column)
 
     def slot_at(by):
         return lax.rem(z + by + layers, layers)
 
     def ring_peer(by):
-        return (slot_at(by) * LAYER + j, h)
+        return ((slot_at(by) * 2 + parity_z) * LAYER + j, h)
 
     right, left = ring_peer(1), ring_peer(-1)
 
@@ -181,37 +211,46 @@
 
     halo_steps = [(dr, dc) for dr in (-1, 0, 1) for dc in (-1, 0, 1) if (dr, dc) != (0, 0)]
     halo_peers = [(shifted(s, dr, seqs), shifted(h, dc, heads)) for dr, dc in halo_steps]
-    partners = [head_peer(i) for i in range(heads)]
-    partners += [layer_peer(i) for i in range(1, LAYER)]
+    partners = [group_peer(i)[0] for i in range(1, heads)]
     partners += [right, left]
+    partners += [part_peer(i) for i in range(1, PAIR)]
+    partners += [share_source(i) for i in range(1, PAIR)]
+    partners += [head_peer(i) for i in range(heads)]
     partners += halo_peers
     for load in loads[:3]:
         load.start()
     barrier = pltpu.get_barrier_semaphore()
     for partner in partners:
         pl.semaphore_signal(barrier, inc=1, device_id=partner, device_id_type=MESH)
+
+    @pl.when(apart == 1)
+    def _():
+        pl.semaphore_signal(barrier, inc=1, device_id=share_source(0), device_id_type=MESH)
+
     group_cols = [slice(g * width, (g + 1) * width) for g in range(heads)]
     for at, whole in enumerate((keys, values)):
         loads[at].wait()
         for g, cols in enumerate(group_cols):
             kv_stage[g, at] = whole[:, cols]
-    pl.semaphore_wait(barrier, len(partners))
+    pl.semaphore_wait(barrier, len(partners) + apart)
 
     def send_kv(i, carry):
-        to = head_peer(i)
-        remote(kv_stage.at[to[1]], kv_in.at[h], kv_send, kv_recv, to).start()
+        to, group = group_peer(i)
+        remote(kv_stage.at[group], kv_in.at[place], kv_send, kv_recv, to).start()
         return carry
 
     def send_q(i, carry):
-        to = head_peer(i)
-        remote(q_stage.at[to[1]], q_in.at[h], q_a2a_send, q_a2a_recv, to).start()
-        return carry
-
-    lax.fori_loop(0, heads, send_kv, 0)
+        to, group = group_peer(i)
+        remote(q_stage.at[group], q_in.at[place], q_a2a_send, q_a2a_recv, to).start()
+        return carry
+
+    lax.fori_loop(1, heads, send_kv, 0)
+    kv_in[place] = kv_stage[place]
     loads[2].wait()
     for g, cols in enumerate(group_cols):
         q_stage[g] = queries[:, cols]
-    lax.fori_loop(0, heads, send_q, 0)
+    lax.fori_loop(1, heads, send_q, 0)
+    q_in[place] = q_stage[place]
     for load in loads[3:7]:
         load.start()
 
@@ -241,7 +280,8 @@
         return block.astype(F32).reshape(rows, width).astype(BF16)
 
     peer = head_peer(0)
-    remote(kv_in, kv_in, kv_send, kv_recv, peer).wait_recv()
+    seven = kv_in.at[pl.ds(0, heads - 1)]
+    remote(seven, seven, kv_send, kv_recv, peer).wait_recv()
     own_k = rows_of(kv_in[:, 0])
     own_v = rows_of(kv_in[:, 1])
     for n in range(GROUP):
@@ -263,12 +303,18 @@
     for load in loads[7:]:
         load.start()
 
-    remote(q_in, q_in, q_a2a_send, q_a2a_recv, peer).wait_recv()
+    seven = q_in.at[pl.ds(0, heads - 1)]
+    remote(seven, seven, q_a2a_send, q_a2a_recv, peer).wait_recv()
     own_q = rows_of(q_in[...])
     for n in range(GROUP):
-        qs[n, r] = own_q[:, n * HEAD_DIM : (n + 1) * HEAD_DIM]
-    for i in range(1, LAYER):
-        remote(qs.at[:, r], qs.at[:, r], q_send, q_recv, layer_peer(i)).start()
+        qs[part_of, n] = own_q[:, n * HEAD_DIM : (n + 1) * HEAD_DIM]
+
+    def send_queries(i, carry):
+        remote(qs.at[part_of], qs.at[part_of], q_send, q_recv, part_peer(i)).start()
+        return carry
+
+    lax.fori_loop(1, PAIR, send_queries, 0)
+
     def weigh(scores, top):
         return jnp.exp2((scores - top) * (SCORE_SCALE * LOG2E))
 
@@ -279,7 +325,8 @@
         keys_now = jnp.concatenate([text_k[mine, cols], kv[z, n, 0]], axis=0)
         values_now = jnp.concatenate([text_v[mine, cols], kv[z, n, 1]], axis=0)
         scores = dot(keys_now, q_turned[n])
-        real = jnp.concatenate([mask_column[mine, :1], jnp.ones((rows, 1), F32)], axis=0) == 1.0
+        held = mask_column[mine, :1] * (1 - apart).astype(F32)
+        real = jnp.concatenate([held, jnp.ones((rows, 1), F32)], axis=0) == 1.0
         real = jnp.broadcast_to(real, scores.shape)
         scores = jnp.where(real, scores, NEG)
         top = jnp.max(scores, axis=0, keepdims=True)
@@ -342,10 +389,21 @@
         lax.fori_loop(0, GROUP, one_head, 0)
 
     pass_on(1)
-    three = qs.at[:, pl.ds(0, LAYER - 1)]
-    remote(three, three, q_send, q_recv, layer_peer(1)).wait_recv()
-    for n in range(GROUP):
-        q_turned[n] = qs[n].reshape(LAYER * rows, HEAD_DIM).T
+    seven = qs.at[pl.ds(0, PAIR - 1)]
+    remote(seven, seven, q_send, q_recv, peer).wait_recv()
+    half = rows // 2
+
+    def turn_queries(n, carry):
+        pieces = [
+            qs[y * LAYER + row, n, at * half : (at + 1) * half]
+            for at in range(2)
+            for row in range(LAYER)
+            for y in range(2)
+        ]
+        q_turned[n] = jnp.concatenate(pieces, axis=0).T
+        return carry
+
+    lax.fori_loop(0, GROUP, turn_queries, 0)
     for load in loads[3:7]:
         load.wait()
     mask_column[...] = jnp.broadcast_to(mask[...].astype(F32), (TOK, mask.shape[1])).T
@@ -353,51 +411,40 @@
     pass_on(2)
     sum_taps()
 
-    def two_parities(first):
-        def one_parity(parity, carry):
-            conv_weights(parity)
-            return carry
-
-        lax.fori_loop(first, first + 2, one_parity, 0)
-
-    two_parities(0)
-    pass_on(3)
-    two_parities(2)
+    def one_parity(parity, carry):
+        conv_weights(parity)
+        return carry
+
+    lax.fori_loop(0, parities, one_parity, 0)
+    pass_on_halves(3)
 
     def middle_step(n, carry):
-        @pl.when(n + 4 < far - 1)
-        def _():
-            pass_on(n + 4)
-
-        work_on(n, range(1, far - 4))
+        work_on(n, range(1, far - 1))
         return carry
 
     lax.fori_loop(0, GROUP, middle_step, 0)
-    pass_on_halves(far - 1)
-
-    def late_step(n, carry):
-        work_on(n, range(far - 4, far - 1))
-        return carry
-
-    lax.fori_loop(0, GROUP, late_step, 0)
 
     opposite = slot_at(far)
     marks[...] = jnp.zeros_like(marks)
-
-    def share_of(i):
-        return shifted(r, i, LAYER)
 
     def last_step(n, carry):
         to_right(kv.at[opposite, n, 0], ring_recv.at[opposite, n, 0]).wait_recv()
         to_left(kv.at[opposite, n, 1], ring_recv.at[opposite, n, 1]).wait_recv()
         top, total, acc = absorb(n, [slot_at(1 - far), slot_at(far - 1), opposite])
         share = (acc / total).T.astype(BF16)
-        for i in range(LAYER):
+        for i in range(PAIR):
             o_stage[i, n] = share[i * rows : (i + 1) * rows]
-        for i in range(1, LAYER):
-            remote(
-                o_stage.at[share_of(i), n], o_in.at[j, n], o_send, o_recv, layer_peer(i)
-            ).start()
+
+        def send_share(i, inner):
+            to, row = row_peer(i)
+
+            @pl.when((i != own_row) | (apart == 1))
+            def _():
+                remote(o_stage.at[row, n], o_in.at[part_of, n], o_send, o_recv, to).start()
+
+            return inner
+
+        lax.fori_loop(0, PAIR, send_share, 0)
         level = top * SCORE_SCALE + jnp.log(total)
         first = level.astype(BF16).astype(F32)
         second = (level - first).astype(BF16).astype(F32)
@@ -409,23 +456,49 @@
     lax.fori_loop(0, GROUP, last_step, 0)
     level_rows = marks[...]
     lanes = mark_stage.shape[2]
-    for i in range(LAYER):
-        turned = level_rows if i == 0 else pltpu.roll(level_rows, (LAYER - i) * rows, 1)
+    for i in range(PAIR):
+        turned = level_rows if i == 0 else pltpu.roll(level_rows, (PAIR - i) * rows, 1)
         mark_stage[i] = turned[:, :lanes].astype(BF16)
-    for i in range(1, LAYER):
-        remote(
-            mark_stage.at[share_of(i)], mark_in.at[j], mark_send, mark_recv, layer_peer(i)
-        ).start()
-    o_in[j] = o_stage[r]
-    mark_in[j] = mark_stage[r]
+
+    def send_marks(i, carry):
+        to, row = row_peer(i)
+
+        @pl.when((i != own_row) | (apart == 1))
+        def _():
+            remote(mark_stage.at[row], mark_in.at[part_of], mark_send, mark_recv, to).start()
+
+        return carry
+
+    lax.fori_loop(0, PAIR, send_marks, 0)
+    own_at = row_peer(own_row)[1]
+
+    @pl.when(apart == 0)
+    def _():
+        o_in[part_of] = o_stage[own_at]
+        mark_in[part_of] = mark_stage[own_at]
 
     for load in loads[7:]:
         load.wait()
-    three = o_in.at[pl.ds(0, LAYER - 1)]
-    remote(three, three, o_send, o_recv, layer_peer(1)).wait_recv()
-    three = mark_in.at[pl.ds(0, LAYER - 1)]
-    remote(three, three, mark_send, mark_recv, layer_peer(1)).wait_recv()
-    level_parts = [mark_in[i].astype(F32) for i in range(LAYER)]
+
+    def await_shares(whole, send, recv, sent):
+        def wait(ref):
+            copy = remote(ref, ref, send, recv, peer)
+            if sent:
+                copy.wait_send()
+            else:
+                copy.wait_recv()
+
+        @pl.when(apart == 1)
+        def _():
+            wait(whole)
+
+        @pl.when(apart == 0)
+        def _():
+            wait(whole.at[pl.ds(0, PAIR - 1)])
+
+    await_shares(o_in, o_send, o_recv, False)
+    await_shares(mark_in, mark_send, mark_recv, False)
+    level_parts = [mark_in[i].astype(F32) for i in range(PAIR)]
     shares[...] = jnp.zeros_like(shares)
     for n in range(GROUP):
         levels = [
@@ -436,15 +509,15 @@
         parts = [jnp.exp(level - top) for level in levels]
         total = functools.reduce(jnp.add, parts)
         for i, part in enumerate(parts):
-            shares[n * LAYER + i : n * LAYER + i + 1] = part / total
+            shares[n * PAIR + i : n * PAIR + i + 1] = part / total
     columns = shares[...].T[:rows]
     attended = []
     for n in range(GROUP):
         mixed = functools.reduce(
             jnp.add,
             [
-                columns[:, n * LAYER + i : n * LAYER + i + 1] * o_in[i, n].astype(F32)
-                for i in range(LAYER)
+                columns[:, n * PAIR + i : n * PAIR + i + 1] * o_in[i, n].astype(F32)
+                for i in range(PAIR)
             ],
         )
         attended.append(mixed.astype(BF16))
@@ -528,20 +601,20 @@
     decoded_copy = pltpu.make_async_copy(decoded, decoded_hbm, out_sem.at[1])
     decoded_copy.start()
 
-    remote(kv_stage, kv_stage, kv_send, kv_recv, peer).wait_send()
-    remote(q_stage, q_stage, q_a2a_send, q_a2a_recv, peer).wait_send()
+    seven = kv_stage.at[pl.ds(0, heads - 1)]
+    remote(seven, seven, kv_send, kv_recv, peer).wait_send()
+    seven = q_stage.at[pl.ds(0, heads - 1)]
+    remote(seven, seven, q_a2a_send, q_a2a_recv, peer).wait_send()
     ring_all = kv.at[pl.ds(0, far - 1)]
     to_right(ring_all, ring_recv.at[0, 0, 0]).wait_send()
     to_left(ring_all, ring_recv.at[0, 0, 0]).wait_send()
     ring_half = kv.at[0, :, 0]
     to_right(ring_half, ring_recv.at[0, 0, 0], 1).wait_send()
     to_left(ring_half, ring_recv.at[0, 0, 0], 1).wait_send()
-    three = qs.at[:, pl.ds(0, LAYER - 1)]
-    remote(three, three, q_send, q_recv, peer).wait_send()
-    three = o_stage.at[pl.ds(0, LAYER - 1)]
-    remote(three, three, o_send, o_recv, peer).wait_send()
-    three = mark_stage.at[pl.ds(0, LAYER - 1)]
-    remote(three, three, mark_send, mark_recv, peer).wait_send()
+    seven = qs.at[pl.ds(0, PAIR - 1)]
+    remote(seven, seven, q_send, q_recv, peer).wait_send()
+    await_shares(o_stage, o_send, o_recv, True)
+    await_shares(mark_stage, mark_send, mark_recv, True)
     for part in range(rs_parts):
         whole = rs_stage.at[part]
         remote(whole, whole, rs_send.at[part], rs_recv.at[part], peer).wait_send()
@@ -585,7 +658,7 @@
     dim = queries.shape[3]
     width = GROUP * HEAD_DIM
     text = text_keys.shape[0]
-    layers = seqs // LAYER
+    layers = seqs // PAIR
     far = layers // 2
     rows = heads * TOK
     features = final_weight.shape[1]
@@ -629,18 +702,18 @@
             pltpu.VMEM((heads, 2, TOK, width), BF16),
             pltpu.VMEM((heads, TOK, width), BF16),
             pltpu.VMEM((layers, GROUP, 2, rows, HEAD_DIM), BF16),
-            pltpu.VMEM((GROUP, LAYER, rows, HEAD_DIM), BF16),
-            pltpu.VMEM((GROUP, HEAD_DIM, LAYER * rows), BF16),
+            pltpu.VMEM((PAIR, GROUP, rows, HEAD_DIM), BF16),
+            pltpu.VMEM((GROUP, HEAD_DIM, PAIR * rows), BF16),
             pltpu.VMEM((text, TOK), F32),
-            pltpu.VMEM((GROUP, TOK, LAYER * rows), F32),
-            pltpu.VMEM((GROUP, TOK, LAYER * rows), F32),
-            pltpu.VMEM((GROUP, HEAD_DIM, LAYER * rows), F32),
-            pltpu.VMEM((16, LAYER * rows), F32),
-            pltpu.VMEM((LAYER, 16, min(HEAD_DIM, LAYER * rows)), BF16),
-            pltpu.VMEM((LAYER, 16, min(HEAD_DIM, LAYER * rows)), BF16),
-            pltpu.VMEM((16, min(HEAD_DIM, LAYER * rows)), F32),
-            pltpu.VMEM((LAYER, GROUP, rows, HEAD_DIM), BF16),
-            pltpu.VMEM((LAYER, GROUP, rows, HEAD_DIM), BF16),
+            pltpu.VMEM((GROUP, TOK, PAIR * rows), F32),
+            pltpu.VMEM((GROUP, TOK, PAIR * rows), F32),
+            pltpu.VMEM((GROUP, HEAD_DIM, PAIR * rows), F32),
+            pltpu.VMEM((16, PAIR * rows), F32),
+            pltpu.VMEM((PAIR, 16, HEAD_DIM), BF16),
+            pltpu.VMEM((PAIR, 16, HEAD_DIM), BF16),
+            pltpu.VMEM((GROUP * PAIR, HEAD_DIM), F32),
+            pltpu.VMEM((PAIR, GROUP, rows, HEAD_DIM), BF16),
+            pltpu.VMEM((PAIR, GROUP, rows, HEAD_DIM), BF16),
             pltpu.VMEM((rs_parts, heads, TOK, dim // rs_parts), BF16),
             pltpu.VMEM((rs_parts, heads, TOK, dim // rs_parts), BF16),
             pltpu.VMEM((TOK, HEAD_DIM), BF16),

time: 67.4 us -> 62.1 us (0.921)
  Pallas kernels: 66.5 us -> 61.2 us
    pallas_call x1, Pallas kernels: 65 us -> 59.8 us  [body(): pl.pallas_call(functools.partial(kernel, seqs, heads), out_shape=results,...]
where the time goes in v8:
time: 62.1 us; the launch traced here: 61.9 us
  Pallas kernels  61.2 us (99%)
  between operations  0.64 us (1%)
    pallas_call x1, Pallas kernels, body(): pl.pallas_call(functools.partial(kernel, seqs, heads), out_shape=results,...  59.8 us
    pallas_call x1, Pallas kernels, body(): pl.pallas_call(hand_over, out_shape=results, in_specs=[anywhere] * 2, out...  1.46 us

profile of v8, /device:TPU:1, one launch (start us, length us, event | category | flops | bytes accessed | tf_op | source)
XLA Modules:
  0.0 61.9 jit_solution(7759730123226035411)
XLA Ops:
  0.6 59.8 %shard_map.167 = (bf16[8,3072]{1,0:T(8,128)(2,1)}, bf16[2,16,512]{2,1,0:T(8,128)(2,1)}) custom-call(bf16[8,3072]{1,0:T(8,128)(2,1)} %bitcast.17, bf16[8,3072]{1,0:T(8,128)(2,1)} %bitcast.18, bf16[8,3072]{1,0:T(8,128)(2,1)} %bitcast.19, bf16[256,384]{1,0:T(8,128)(2,1)} %text_k_hbm.1, bf16[256,384]{1,0:T(8,128)(2,1)} %text_v_hbm.1, s32[1,256]{1,0:T(1,128)} %bitcast.28, ...), custom_call_target="tpu_custom_call" | custom-call | flops 1200000000 | bytes 5000000 | tf_op jit(solution)/shard_map/pallas_call | solution.py:693
  60.4 1.5 %shard_map.168 = (bf16[8,3072]{1,0:T(8,128)(2,1)}, bf16[2,16,512]{2,1,0:T(8,128)(2,1)}) custom-call(bf16[8,3072]{1,0:T(8,128)(2,1)} %get-tuple-element.6.block_in, bf16[2,16,512]{2,1,0:T(8,128)(2,1)} %get-tuple-element.7.decoded_in), custom_call_target="tpu_custom_call" | custom-call | tf_op jit(solution)/shard_map/pallas_call | solution.py:753

commit v9 on v8

--- a/solution.py
+++ b/solution.py
@@ -145,12 +145,6 @@
     def head_peer(i):
         return (depth * LAYER + r, shifted(h, i, heads))
 
-    def group_peer(i):
-        at_depth = z * 2 + lax.rem(parity_z + i // COLUMNS, 2)
-        at_column = lax.rem(column + lax.rem(i, COLUMNS), COLUMNS)
-        group = lax.rem(at_depth, 2) * COLUMNS + at_column
-        return (at_depth * LAYER + j, y_high * COLUMNS + at_column), group
-
     def part_peer(i):
         part = lax.rem(part_of + i, PAIR)
         return (depth * LAYER + lax.rem(part, LAYER), (part // LAYER) * COLUMNS + column)
@@ -171,6 +165,12 @@
 
     def slot_at(by):
         return lax.rem(z + by + layers, layers)
+
+    def group_peer(i, by=0):
+        at_depth = slot_at(by) * 2 + lax.rem(parity_z + i // COLUMNS, 2)
+        at_column = lax.rem(column + lax.rem(i, COLUMNS), COLUMNS)
+        group = lax.rem(at_depth, 2) * COLUMNS + at_column
+        return (at_depth * LAYER + j, y_high * COLUMNS + at_column), group
 
     def ring_peer(by):
         return ((slot_at(by) * 2 + parity_z) * LAYER + j, h)
@@ -212,7 +212,7 @@
     halo_steps = [(dr, dc) for dr in (-1, 0, 1) for dc in (-1, 0, 1) if (dr, dc) != (0, 0)]
     halo_peers = [(shifted(s, dr, seqs), shifted(h, dc, heads)) for dr, dc in halo_steps]
     partners = [group_peer(i)[0] for i in range(1, heads)]
-    partners += [right, left]
+    partners += [group_peer(i, by)[0] for by in (1, -1) for i in range(heads)]
     partners += [part_peer(i) for i in range(1, PAIR)]
     partners += [share_source(i) for i in range(1, PAIR)]
     partners += [head_peer(i) for i in range(heads)]
@@ -234,18 +234,23 @@
             kv_stage[g, at] = whole[:, cols]
     pl.semaphore_wait(barrier, len(partners) + apart)
 
-    def send_kv(i, carry):
-        to, group = group_peer(i)
-        remote(kv_stage.at[group], kv_in.at[place], kv_send, kv_recv, to).start()
-        return carry
+    sides = ((1, 1), (2, -1), (0, 0))
+    for at, by in sides:
+        def send_kv(i, carry, at=at, by=by):
+            to, group = group_peer(i, by)
+            remote(
+                kv_stage.at[group], kv_in.at[at, place], kv_send.at[at], kv_recv.at[at], to
+            ).start()
+            return carry
+
+        lax.fori_loop(0 if by else 1, heads, send_kv, 0)
+    kv_in[0, place] = kv_stage[place]
 
     def send_q(i, carry):
         to, group = group_peer(i)
         remote(q_stage.at[group], q_in.at[place], q_a2a_send, q_a2a_recv, to).start()
         return carry
 
-    lax.fori_loop(1, heads, send_kv, 0)
-    kv_in[place] = kv_stage[place]
     loads[2].wait()
     for g, cols in enumerate(group_cols):
         q_stage[g] = queries[:, cols]
@@ -280,14 +285,15 @@
         return block.astype(F32).reshape(rows, width).astype(BF16)
 
     peer = head_peer(0)
-    seven = kv_in.at[pl.ds(0, heads - 1)]
-    remote(seven, seven, kv_send, kv_recv, peer).wait_recv()
-    own_k = rows_of(kv_in[:, 0])
-    own_v = rows_of(kv_in[:, 1])
-    for n in range(GROUP):
-        cols = slice(n * HEAD_DIM, (n + 1) * HEAD_DIM)
-        kv[z, n, 0] = own_k[:, cols]
-        kv[z, n, 1] = own_v[:, cols]
+
+    def settle(at, by):
+        came = kv_in.at[at] if by else kv_in.at[at, pl.ds(0, heads - 1)]
+        remote(came, came, kv_send.at[at], kv_recv.at[at], peer).wait_recv()
+        slot = slot_at(by)
+        for part in range(2):
+            whole = rows_of(kv_in[at, :, part])
+            for n in range(GROUP):
+                kv[slot, n, part] = whole[:, n * HEAD_DIM : (n + 1) * HEAD_DIM]
 
     def to_right(ref, recv, send=0):
         return remote(ref, ref, ring_send.at[0] if send == 0 else half_send.at[0], recv, right)
@@ -297,9 +303,15 @@
 
     pieces_of = [(n, part) for n in range(GROUP) for part in range(2)]
 
+    settle(1, -1)
     for n, part in pieces_of:
-        to_right(kv.at[z, n, part], ring_recv.at[z, n, part]).start()
-        to_left(kv.at[z, n, part], ring_recv.at[z, n, part]).start()
+        ref = kv.at[slot_at(-1), n, part]
+        to_right(ref, ring_recv.at[slot_at(-1), n, part]).start()
+    settle(2, 1)
+    for n, part in pieces_of:
+        ref = kv.at[slot_at(1), n, part]
+        to_left(ref, ring_recv.at[slot_at(1), n, part]).start()
+    settle(0, 0)
     for load in loads[7:]:
         load.start()
 
@@ -388,7 +400,6 @@
 
         lax.fori_loop(0, GROUP, one_head, 0)
 
-    pass_on(1)
     seven = qs.at[pl.ds(0, PAIR - 1)]
     remote(seven, seven, q_send, q_recv, peer).wait_recv()
     half = rows // 2
@@ -601,11 +612,12 @@
     decoded_copy = pltpu.make_async_copy(decoded, decoded_hbm, out_sem.at[1])
     decoded_copy.start()
 
-    seven = kv_stage.at[pl.ds(0, heads - 1)]
-    remote(seven, seven, kv_send, kv_recv, peer).wait_send()
+    for at, by in sides:
+        gone = kv_stage if by else kv_stage.at[pl.ds(0, heads - 1)]
+        remote(gone, gone, kv_send.at[at], kv_recv.at[at], peer).wait_send()
     seven = q_stage.at[pl.ds(0, heads - 1)]
     remote(seven, seven, q_a2a_send, q_a2a_recv, peer).wait_send()
-    ring_all = kv.at[pl.ds(0, far - 1)]
+    ring_all = kv.at[pl.ds(0, far - 2)]
     to_right(ring_all, ring_recv.at[0, 0, 0]).wait_send()
     to_left(ring_all, ring_recv.at[0, 0, 0]).wait_send()
     ring_half = kv.at[0, :, 0]
@@ -699,7 +711,7 @@
         + [
             pltpu.VMEM((heads, 2, TOK, width), BF16),
             pltpu.VMEM((heads, TOK, width), BF16),
-            pltpu.VMEM((heads, 2, TOK, width), BF16),
+            pltpu.VMEM((3, heads, 2, TOK, width), BF16),
             pltpu.VMEM((heads, TOK, width), BF16),
             pltpu.VMEM((layers, GROUP, 2, rows, HEAD_DIM), BF16),
             pltpu.VMEM((PAIR, GROUP, rows, HEAD_DIM), BF16),
@@ -725,8 +737,8 @@
             pltpu.VMEM((2, 2 * TOK, channels), BF16),
             dma((len(operands),)),
             dma((2,)),
-            dma,
-            dma,
+            dma((3,)),
+            dma((3,)),
             dma,
             dma,
             dma((2,)),

time: 62.1 us -> 65 us (1.047)
  Pallas kernels: 61.2 us -> 64.1 us
    pallas_call x1, Pallas kernels: 59.8 us -> 62.6 us  [body(): pl.pallas_call(functools.partial(kernel, seqs, heads), out_shape=results,...]
where the time goes in v9:
time: 65 us; the launch traced here: 64.7 us
  Pallas kernels  64.1 us (99%)
    pallas_call x1, Pallas kernels, body(): pl.pallas_call(functools.partial(kernel, seqs, heads), out_shape=results,...  62.6 us
    pallas_call x1, Pallas kernels, body(): pl.pallas_call(hand_over, out_shape=results, in_specs=[anywhere] * 2, out...  1.46 us

profile of v9, /device:TPU:1, one launch (start us, length us, event | category | flops | bytes accessed | tf_op | source)
XLA Modules:
  0.0 64.7 jit_solution(7390349793330395370)
XLA Ops:
  0.6 62.6 %shard_map.167 = (bf16[8,3072]{1,0:T(8,128)(2,1)}, bf16[2,16,512]{2,1,0:T(8,128)(2,1)}) custom-call(bf16[8,3072]{1,0:T(8,128)(2,1)} %bitcast.17, bf16[8,3072]{1,0:T(8,128)(2,1)} %bitcast.18, bf16[8,3072]{1,0:T(8,128)(2,1)} %bitcast.19, bf16[256,384]{1,0:T(8,128)(2,1)} %text_k_hbm.1, bf16[256,384]{1,0:T(8,128)(2,1)} %text_v_hbm.1, s32[1,256]{1,0:T(1,128)} %bitcast.28, ...), custom_call_target="tpu_custom_call" | custom-call | flops 1200000000 | bytes 5000000 | tf_op jit(solution)/shard_map/pallas_call | solution.py:705
  63.3 1.5 %shard_map.168 = (bf16[8,3072]{1,0:T(8,128)(2,1)}, bf16[2,16,512]{2,1,0:T(8,128)(2,1)}) custom-call(bf16[8,3072]{1,0:T(8,128)(2,1)} %get-tuple-element.6.block_in, bf16[2,16,512]{2,1,0:T(8,128)(2,1)} %get-tuple-element.7.decoded_in), custom_call_target="tpu_custom_call" | custom-call | tf_op jit(solution)/shard_map/pallas_call | solution.py:765

commit v10 on v8

--- a/solution.py
+++ b/solution.py
@@ -84,8 +84,6 @@
     run_sum,
     run_acc,
     marks,
-    mark_stage,
-    mark_in,
     shares,
     o_stage,
     o_in,
@@ -111,8 +109,6 @@
     q_recv,
     o_send,
     o_recv,
-    mark_send,
-    mark_recv,
     rs_send,
     rs_recv,
     halo_send,
@@ -164,11 +160,6 @@
 
     own_row = LAYER // 2
 
-    def share_source(i):
-        part = lax.rem(part_of + i, PAIR)
-        at = (z * 2 + y_high) * LAYER + lax.rem(part, LAYER)
-        return (at, (part // LAYER) * COLUMNS + column)
-
     def slot_at(by):
         return lax.rem(z + by + layers, layers)
 
@@ -214,8 +205,6 @@
     partners = [group_peer(i)[0] for i in range(1, heads)]
     partners += [right, left]
     partners += [part_peer(i) for i in range(1, PAIR)]
-    partners += [share_source(i) for i in range(1, PAIR)]
-    partners += [head_peer(i) for i in range(heads)]
     partners += halo_peers
     for load in loads[:3]:
         load.start()
@@ -223,16 +212,12 @@
     for partner in partners:
         pl.semaphore_signal(barrier, inc=1, device_id=partner, device_id_type=MESH)
 
-    @pl.when(apart == 1)
-    def _():
-        pl.semaphore_signal(barrier, inc=1, device_id=share_source(0), device_id_type=MESH)
-
     group_cols = [slice(g * width, (g + 1) * width) for g in range(heads)]
     for at, whole in enumerate((keys, values)):
         loads[at].wait()
         for g, cols in enumerate(group_cols):
             kv_stage[g, at] = whole[:, cols]
-    pl.semaphore_wait(barrier, len(partners) + apart)
+    pl.semaphore_wait(barrier, len(partners))
 
     def send_kv(i, carry):
         to, group = group_peer(i)
@@ -295,11 +280,9 @@
     def to_left(ref, recv, send=0):
         return remote(ref, ref, ring_send.at[1] if send == 0 else half_send.at[1], recv, left)
 
-    pieces_of = [(n, part) for n in range(GROUP) for part in range(2)]
-
-    for n, part in pieces_of:
-        to_right(kv.at[z, n, part], ring_recv.at[z, n, part]).start()
-        to_left(kv.at[z, n, part], ring_recv.at[z, n, part]).start()
+    for n in range(GROUP):
+        to_right(kv.at[z, n], ring_recv.at[z, n, 0]).start()
+        to_left(kv.at[z, n], ring_recv.at[z, n, 0]).start()
     for load in loads[7:]:
         load.start()
 
@@ -359,13 +342,12 @@
         other = slot_at(step)
 
         def one_head(n, carry):
-            for part in range(2):
-                copy = to_right(kv.at[one, n, part], ring_recv.at[one, n, part])
-                copy.wait_recv()
-                copy.start()
-                copy = to_left(kv.at[other, n, part], ring_recv.at[other, n, part])
-                copy.wait_recv()
-                copy.start()
+            copy = to_right(kv.at[one, n], ring_recv.at[one, n, 0])
+            copy.wait_recv()
+            copy.start()
+            copy = to_left(kv.at[other, n], ring_recv.at[other, n, 0])
+            copy.wait_recv()
+            copy.start()
             return carry
 
         lax.fori_loop(0, GROUP, one_head, 0)
@@ -375,15 +357,10 @@
         other = slot_at(step)
 
         def one_head(n, carry):
-            for part in range(2):
-                copy = to_right(kv.at[one, n, part], ring_recv.at[one, n, part], 1)
-                copy.wait_recv()
-                if part == 0:
-                    copy.start()
-                copy = to_left(kv.at[other, n, part], ring_recv.at[other, n, part], 1)
-                copy.wait_recv()
-                if part == 1:
-                    copy.start()
+            to_right(kv.at[one, n], ring_recv.at[one, n, 0]).wait_recv()
+            to_right(kv.at[one, n, 0], ring_recv.at[one, n, 0], 1).start()
+            to_left(kv.at[other, n], ring_recv.at[other, n, 0]).wait_recv()
+            to_left(kv.at[other, n, 1], ring_recv.at[other, n, 1], 1).start()
             return carry
 
         lax.fori_loop(0, GROUP, one_head, 0)
@@ -433,18 +410,9 @@
         top, total, acc = absorb(n, [slot_at(1 - far), slot_at(far - 1), opposite])
         share = (acc / total).T.astype(BF16)
         for i in range(PAIR):
-            o_stage[i, n] = share[i * rows : (i + 1) * rows]
-
-        def send_share(i, inner):
-            to, row = row_peer(i)
-
-            @pl.when((i != own_row) | (apart == 1))
-            def _():
-                remote(o_stage.at[row, n], o_in.at[part_of, n], o_send, o_recv, to).start()
-
-            return inner
-
-        lax.fori_loop(0, PAIR, send_share, 0)
+            o_stage[i, pl.ds(pl.multiple_of(n * rows, rows), rows)] = share[
+                i * rows : (i + 1) * rows
+            ]
         level = top * SCORE_SCALE + jnp.log(total)
         first = level.astype(BF16).astype(F32)
         second = (level - first).astype(BF16).astype(F32)
@@ -455,27 +423,25 @@
 
     lax.fori_loop(0, GROUP, last_step, 0)
     level_rows = marks[...]
-    lanes = mark_stage.shape[2]
     for i in range(PAIR):
         turned = level_rows if i == 0 else pltpu.roll(level_rows, (PAIR - i) * rows, 1)
-        mark_stage[i] = turned[:, :lanes].astype(BF16)
-
-    def send_marks(i, carry):
+        o_stage[i, GROUP * rows :] = turned[:, :HEAD_DIM].astype(BF16)
+
+    def send_share(i, carry):
         to, row = row_peer(i)
 
         @pl.when((i != own_row) | (apart == 1))
         def _():
-            remote(mark_stage.at[row], mark_in.at[part_of], mark_send, mark_recv, to).start()
-
-        return carry
-
-    lax.fori_loop(0, PAIR, send_marks, 0)
+            remote(o_stage.at[row], o_in.at[part_of], o_send, o_recv, to).start()
+
+        return carry
+
+    lax.fori_loop(0, PAIR, send_share, 0)
     own_at = row_peer(own_row)[1]
 
     @pl.when(apart == 0)
     def _():
         o_in[part_of] = o_stage[own_at]
-        mark_in[part_of] = mark_stage[own_at]
 
     for load in loads[7:]:
         load.wait()
@@ -497,8 +463,7 @@
             wait(whole.at[pl.ds(0, PAIR - 1)])
 
     await_shares(o_in, o_send, o_recv, False)
-    await_shares(mark_in, mark_send, mark_recv, False)
-    level_parts = [mark_in[i].astype(F32) for i in range(PAIR)]
+    level_parts = [o_in[i, GROUP * rows :].astype(F32) for i in range(PAIR)]
     shares[...] = jnp.zeros_like(shares)
     for n in range(GROUP):
         levels = [
@@ -516,7 +481,7 @@
         mixed = functools.reduce(
             jnp.add,
             [
-                columns[:, n * PAIR + i : n * PAIR + i + 1] * o_in[i, n].astype(F32)
+                columns[:, n * PAIR + i : n * PAIR + i + 1] * o_in[i, n * rows : (n + 1) * rows].astype(F32)
                 for i in range(PAIR)
             ],
         )
@@ -614,7 +579,6 @@
     seven = qs.at[pl.ds(0, PAIR - 1)]
     remote(seven, seven, q_send, q_recv, peer).wait_send()
     await_shares(o_stage, o_send, o_recv, True)
-    await_shares(mark_stage, mark_send, mark_recv, True)
     for part in range(rs_parts):
         whole = rs_stage.at[part]
         remote(whole, whole, rs_send.at[part], rs_recv.at[part], peer).wait_send()
@@ -664,7 +628,7 @@
     features = final_weight.shape[1]
     taps = 9 * LAT_CH
     channels = conv_weight.shape[4]
-    rs_parts = 2
+    rs_parts = 1
     operands = (
         queries.reshape(TOK, dim),
         keys.reshape(TOK, dim),
@@ -709,11 +673,9 @@
             pltpu.VMEM((GROUP, TOK, PAIR * rows), F32),
             pltpu.VMEM((GROUP, HEAD_DIM, PAIR * rows), F32),
             pltpu.VMEM((16, PAIR * rows), F32),
-            pltpu.VMEM((PAIR, 16, HEAD_DIM), BF16),
-            pltpu.VMEM((PAIR, 16, HEAD_DIM), BF16),
             pltpu.VMEM((GROUP * PAIR, HEAD_DIM), F32),
-            pltpu.VMEM((PAIR, GROUP, rows, HEAD_DIM), BF16),
-            pltpu.VMEM((PAIR, GROUP, rows, HEAD_DIM), BF16),
+            pltpu.VMEM((PAIR, GROUP * rows + 16, HEAD_DIM), BF16),
+            pltpu.VMEM((PAIR, GROUP * rows + 16, HEAD_DIM), BF16),
             pltpu.VMEM((rs_parts, heads, TOK, dim // rs_parts), BF16),
             pltpu.VMEM((rs_parts, heads, TOK, dim // rs_parts), BF16),
             pltpu.VMEM((TOK, HEAD_DIM), BF16),
@@ -732,8 +694,6 @@
             dma((2,)),
             dma((2,)),
             dma((layers, GROUP, 2)),
-            dma,
-            dma,
             dma,
             dma,
             dma,

time: 62.1 us -> 63.4 us (1.021)
  Pallas kernels: 61.2 us -> 62.5 us
    pallas_call x1, Pallas kernels: 59.8 us -> 61 us  [body(): pl.pallas_call(functools.partial(kernel, seqs, heads), out_shape=results,...]
where the time goes in v10:
time: 63.4 us; the launch traced here: 63.1 us
  Pallas kernels  62.5 us (99%)
  between operations  0.64 us (1%)
    pallas_call x1, Pallas kernels, body(): pl.pallas_call(functools.partial(kernel, seqs, heads), out_shape=results,...  61 us
    pallas_call x1, Pallas kernels, body(): pl.pallas_call(hand_over, out_shape=results, in_specs=[anywhere] * 2, out...  1.46 us

profile of v10, /device:TPU:1, one launch (start us, length us, event | category | flops | bytes accessed | tf_op | source)
XLA Modules:
  0.0 63.1 jit_solution(5663957107625241306)
XLA Ops:
  0.6 61.0 %shard_map.167 = (bf16[8,3072]{1,0:T(8,128)(2,1)}, bf16[2,16,512]{2,1,0:T(8,128)(2,1)}) custom-call(bf16[8,3072]{1,0:T(8,128)(2,1)} %bitcast.17, bf16[8,3072]{1,0:T(8,128)(2,1)} %bitcast.18, bf16[8,3072]{1,0:T(8,128)(2,1)} %bitcast.19, bf16[256,384]{1,0:T(8,128)(2,1)} %text_k_hbm.1, bf16[256,384]{1,0:T(8,128)(2,1)} %text_v_hbm.1, s32[1,256]{1,0:T(1,128)} %bitcast.28, ...), custom_call_target="tpu_custom_call" | custom-call | flops 1200000000 | bytes 5000000 | tf_op jit(solution)/shard_map/pallas_call | solution.py:657
  61.7 1.5 %shard_map.168 = (bf16[8,3072]{1,0:T(8,128)(2,1)}, bf16[2,16,512]{2,1,0:T(8,128)(2,1)}) custom-call(bf16[8,3072]{1,0:T(8,128)(2,1)} %get-tuple-element.6.block_in, bf16[2,16,512]{2,1,0:T(8,128)(2,1)} %get-tuple-element.7.decoded_in), custom_call_target="tpu_custom_call" | custom-call | tf_op jit(solution)/shard_map/pallas_call | solution.py:713

commit v11 on v8

--- a/solution.py
+++ b/solution.py
@@ -164,11 +164,6 @@
 
     own_row = LAYER // 2
 
-    def share_source(i):
-        part = lax.rem(part_of + i, PAIR)
-        at = (z * 2 + y_high) * LAYER + lax.rem(part, LAYER)
-        return (at, (part // LAYER) * COLUMNS + column)
-
     def slot_at(by):
         return lax.rem(z + by + layers, layers)
 
@@ -214,8 +209,6 @@
     partners = [group_peer(i)[0] for i in range(1, heads)]
     partners += [right, left]
     partners += [part_peer(i) for i in range(1, PAIR)]
-    partners += [share_source(i) for i in range(1, PAIR)]
-    partners += [head_peer(i) for i in range(heads)]
     partners += halo_peers
     for load in loads[:3]:
         load.start()
@@ -223,16 +216,12 @@
     for partner in partners:
         pl.semaphore_signal(barrier, inc=1, device_id=partner, device_id_type=MESH)
 
-    @pl.when(apart == 1)
-    def _():
-        pl.semaphore_signal(barrier, inc=1, device_id=share_source(0), device_id_type=MESH)
-
     group_cols = [slice(g * width, (g + 1) * width) for g in range(heads)]
     for at, whole in enumerate((keys, values)):
         loads[at].wait()
         for g, cols in enumerate(group_cols):
             kv_stage[g, at] = whole[:, cols]
-    pl.semaphore_wait(barrier, len(partners) + apart)
+    pl.semaphore_wait(barrier, len(partners))
 
     def send_kv(i, carry):
         to, group = group_peer(i)
@@ -664,7 +653,7 @@
     features = final_weight.shape[1]
     taps = 9 * LAT_CH
     channels = conv_weight.shape[4]
-    rs_parts = 2
+    rs_parts = 4
     operands = (
         queries.reshape(TOK, dim),
         keys.reshape(TOK, dim),

time: 62.1 us -> 62.1 us (level)
  no operation moved by 1% of the time
where the time goes in v11:
time: 62.1 us; the launch traced here: 61.9 us
  Pallas kernels  61.2 us (99%)
  between operations  0.64 us (1%)
    pallas_call x1, Pallas kernels, body(): pl.pallas_call(functools.partial(kernel, seqs, heads), out_shape=results,...  59.8 us
    pallas_call x1, Pallas kernels, body(): pl.pallas_call(hand_over, out_shape=results, in_specs=[anywhere] * 2, out...  1.46 us

profile of v11, /device:TPU:1, one launch (start us, length us, event | category | flops | bytes accessed | tf_op | source)
XLA Modules:
  0.0 61.9 jit_solution(16723031358971746961)
XLA Ops:
  0.6 59.8 %shard_map.167 = (bf16[8,3072]{1,0:T(8,128)(2,1)}, bf16[2,16,512]{2,1,0:T(8,128)(2,1)}) custom-call(bf16[8,3072]{1,0:T(8,128)(2,1)} %bitcast.17, bf16[8,3072]{1,0:T(8,128)(2,1)} %bitcast.18, bf16[8,3072]{1,0:T(8,128)(2,1)} %bitcast.19, bf16[256,384]{1,0:T(8,128)(2,1)} %text_k_hbm.1, bf16[256,384]{1,0:T(8,128)(2,1)} %text_v_hbm.1, s32[1,256]{1,0:T(1,128)} %bitcast.28, ...), custom_call_target="tpu_custom_call" | custom-call | flops 1200000000 | bytes 5000000 | tf_op jit(solution)/shard_map/pallas_call | solution.py:682
  60.4 1.5 %shard_map.168 = (bf16[8,3072]{1,0:T(8,128)(2,1)}, bf16[2,16,512]{2,1,0:T(8,128)(2,1)}) custom-call(bf16[8,3072]{1,0:T(8,128)(2,1)} %get-tuple-element.6.block_in, bf16[2,16,512]{2,1,0:T(8,128)(2,1)} %get-tuple-element.7.decoded_in), custom_call_target="tpu_custom_call" | custom-call | tf_op jit(solution)/shard_map/pallas_call | solution.py:742

commit v12 on v11

--- a/solution.py
+++ b/solution.py
@@ -54,8 +54,8 @@
     final_bias_hbm,
     conv_w_hbm,
     conv_bias_hbm,
-    block_hbm,
-    decoded_hbm,
+    block_out,
+    decoded,
     queries,
     keys,
     values,
@@ -96,10 +96,7 @@
     w_sum,
     w_full,
     pixels,
-    block_out,
-    decoded,
     local_sem,
-    out_sem,
     kv_send,
     kv_recv,
     q_a2a_send,
@@ -538,8 +535,6 @@
         rounded = stream.astype(BF16)
         block_out[:, cols] = rounded
         pieces.append(rounded.astype(F32))
-    block_copy = pltpu.make_async_copy(block_out, block_hbm, out_sem.at[0])
-    block_copy.start()
 
     normed_in = jnp.concatenate(pieces, axis=1)
     centered = normed_in - jnp.mean(normed_in, axis=1, keepdims=True)
@@ -587,8 +582,6 @@
     for tile in range(pixels.shape[1]):
         cols = slice(tile * HEAD_DIM, (tile + 1) * HEAD_DIM)
         decoded[:, :, cols] = pixels[:, tile].astype(BF16)
-    decoded_copy = pltpu.make_async_copy(decoded, decoded_hbm, out_sem.at[1])
-    decoded_copy.start()
 
     seven = kv_stage.at[pl.ds(0, heads - 1)]
     remote(seven, seven, kv_send, kv_recv, peer).wait_send()
@@ -608,21 +601,17 @@
         whole = rs_stage.at[part]
         remote(whole, whole, rs_send.at[part], rs_recv.at[part], peer).wait_send()
     remote(halo, halo, halo_send, halo_recv, peer).wait_send()
-    block_copy.wait()
-    decoded_copy.wait()
-
-
-def hand_over(block_in, decoded_in, block_to, decoded_to, block, decoded, sem):
-    rooms = ((block_in, block, block_to), (decoded_in, decoded, decoded_to))
-    loads = [pltpu.make_async_copy(a, b, sem.at[i]) for i, (a, b, _) in enumerate(rooms)]
-    stores = [pltpu.make_async_copy(b, c, sem.at[2 + i]) for i, (_, b, c) in enumerate(rooms)]
-    for load in loads:
-        load.start()
-    for load, store in zip(loads, stores):
-        load.wait()
-        store.start()
-    for store in stores:
-        store.wait()
+
+
+def hand_over(block_in, decoded_in, block_to, decoded_to, sem):
+    copies = [
+        pltpu.make_async_copy(block_in, block_to, sem.at[0]),
+        pltpu.make_async_copy(decoded_in, decoded_to, sem.at[1]),
+    ]
+    for copy in copies:
+        copy.start()
+    for copy in copies:
+        copy.wait()
 
 
 def body(seqs, heads, *args):
@@ -679,11 +668,12 @@
         jax.ShapeDtypeStruct((TOK, dim), BF16),
         jax.ShapeDtypeStruct((2, 2 * TOK, channels), BF16),
     )
+    held = pl.BlockSpec(memory_space=pltpu.VMEM)
     block_out, decoded = pl.pallas_call(
         functools.partial(kernel, seqs, heads),
-        out_shape=results,
+        out_shape=tuple(pltpu.VMEM(x.shape, x.dtype) for x in results),
         in_specs=[anywhere] * len(operands),
-        out_specs=(anywhere, anywhere),
+        out_specs=(held, held),
         scratch_shapes=copied
         + [
             pltpu.VMEM((heads, 2, TOK, width), BF16),
@@ -710,10 +700,7 @@
             pltpu.VMEM((taps, channels), BF16),
             pltpu.VMEM((4, 4 * features, channels), BF16),
             pltpu.VMEM((2, channels // HEAD_DIM, 2 * TOK, HEAD_DIM), F32),
-            pltpu.VMEM((TOK, dim), BF16),
-            pltpu.VMEM((2, 2 * TOK, channels), BF16),
             dma((len(operands),)),
-            dma((2,)),
             dma,
             dma,
             dma,
@@ -742,10 +729,10 @@
     block_out, decoded = pl.pallas_call(
         hand_over,
         out_shape=results,
-        in_specs=[anywhere] * 2,
+        in_specs=(anywhere, anywhere),
         out_specs=(anywhere, anywhere),
-        scratch_shapes=[pltpu.VMEM(x.shape, x.dtype) for x in results] + [dma((4,))],
-        compiler_params=pltpu.CompilerParams(vmem_limit_bytes=60 * 1024 * 1024),
+        scratch_shapes=[dma((2,))],
+        compiler_params=pltpu.CompilerParams(vmem_limit_bytes=2 * 1024 * 1024),
     )(block_out, decoded)
     return (
         block_out.reshape(1, TOK, 1, dim),

time: 62.1 us -> 60.6 us (0.976)
  Pallas kernels: 61.2 us -> 59.8 us
    pallas_call x2, Pallas kernels: 61.2 us -> 59.8 us  [the longest x1 59.2 us: body(): pl.pallas_call(functools.partial(kernel, seqs, heads), out_shape=tuple((p...]
where the time goes in v12:
time: 60.6 us; the launch traced here: 60.5 us
  Pallas kernels  59.8 us (99%)
  between operations  0.64 us (1%)
    pallas_call x1, Pallas kernels, body(): pl.pallas_call(functools.partial(kernel, seqs, heads), out_shape=tuple((p...  59.2 us

profile of v12, /device:TPU:1, one launch (start us, length us, event | category | flops | bytes accessed | tf_op | source)
XLA Modules:
  0.0 60.5 jit_solution(15107503457647454032)
XLA Ops:
  0.6 59.2 %shard_map.167 = (bf16[8,3072]{1,0:T(8,128)(2,1)S(1)}, bf16[2,16,512]{2,1,0:T(8,128)(2,1)S(1)}) custom-call(bf16[8,3072]{1,0:T(8,128)(2,1)} %bitcast.17, bf16[8,3072]{1,0:T(8,128)(2,1)} %bitcast.18, bf16[8,3072]{1,0:T(8,128)(2,1)} %bitcast.19, bf16[256,384]{1,0:T(8,128)(2,1)} %text_k_hbm.1, bf16[256,384]{1,0:T(8,128)(2,1)} %text_v_hbm.1, s32[1,256]{1,0:T(1,128)} %bitcast.28, ...), custom_call_target="tpu_custom_call" | custom-call | flops 1200000000 | bytes 5000000 | tf_op jit(solution)/shard_map/pallas_call | solution.py:672
  59.8 0.7 %shard_map.168 = (bf16[8,3072]{1,0:T(8,128)(2,1)}, bf16[2,16,512]{2,1,0:T(8,128)(2,1)}) custom-call(bf16[8,3072]{1,0:T(8,128)(2,1)S(1)} %get-tuple-element.6.block_in, bf16[2,16,512]{2,1,0:T(8,128)(2,1)S(1)} %get-tuple-element.7.decoded_in), custom_call_target="tpu_custom_call" | custom-call | tf_op jit(solution)/shard_map/pallas_call | solution.py:729

commit v13 on v12

--- a/solution.py
+++ b/solution.py
@@ -206,7 +206,6 @@
     partners = [group_peer(i)[0] for i in range(1, heads)]
     partners += [right, left]
     partners += [part_peer(i) for i in range(1, PAIR)]
-    partners += halo_peers
     for load in loads[:3]:
         load.start()
     barrier = pltpu.get_barrier_semaphore()
@@ -405,7 +404,7 @@
     pass_on_halves(3)
 
     def middle_step(n, carry):
-        work_on(n, range(1, far - 1))
+        work_on(n, range(1, far))
         return carry
 
     lax.fori_loop(0, GROUP, middle_step, 0)
@@ -416,7 +415,7 @@
     def last_step(n, carry):
         to_right(kv.at[opposite, n, 0], ring_recv.at[opposite, n, 0]).wait_recv()
         to_left(kv.at[opposite, n, 1], ring_recv.at[opposite, n, 1]).wait_recv()
-        top, total, acc = absorb(n, [slot_at(1 - far), slot_at(far - 1), opposite])
+        top, total, acc = absorb(n, [opposite])
         share = (acc / total).T.astype(BF16)
         for i in range(PAIR):
             o_stage[i, n] = share[i * rows : (i + 1) * rows]

time: 60.6 us -> 59.8 us (0.987)
  Pallas kernels: 59.8 us -> 59 us
    pallas_call x1, Pallas kernels: 59.2 us -> 58.3 us  [body(): pl.pallas_call(functools.partial(kernel, seqs, heads), out_shape=tuple((p...]
where the time goes in v13:
time: 59.8 us; the launch traced here: 59.6 us
  Pallas kernels  59 us (99%)
  between operations  0.64 us (1%)
    pallas_call x1, Pallas kernels, body(): pl.pallas_call(functools.partial(kernel, seqs, heads), out_shape=tuple((p...  58.3 us

profile of v13, /device:TPU:1, one launch (start us, length us, event | category | flops | bytes accessed | tf_op | source)
XLA Modules:
  0.0 59.6 jit_solution(18229934380944122306)
XLA Ops:
  0.6 58.3 %shard_map.167 = (bf16[8,3072]{1,0:T(8,128)(2,1)S(1)}, bf16[2,16,512]{2,1,0:T(8,128)(2,1)S(1)}) custom-call(bf16[8,3072]{1,0:T(8,128)(2,1)} %bitcast.17, bf16[8,3072]{1,0:T(8,128)(2,1)} %bitcast.18, bf16[8,3072]{1,0:T(8,128)(2,1)} %bitcast.19, bf16[256,384]{1,0:T(8,128)(2,1)} %text_k_hbm.1, bf16[256,384]{1,0:T(8,128)(2,1)} %text_v_hbm.1, s32[1,256]{1,0:T(1,128)} %bitcast.28, ...), custom_call_target="tpu_custom_call" | custom-call | flops 1200000000 | bytes 5000000 | tf_op jit(solution)/shard_map/pallas_call | solution.py:671
  59.0 0.7 %shard_map.168 = (bf16[8,3072]{1,0:T(8,128)(2,1)}, bf16[2,16,512]{2,1,0:T(8,128)(2,1)}) custom-call(bf16[8,3072]{1,0:T(8,128)(2,1)S(1)} %get-tuple-element.6.block_in, bf16[2,16,512]{2,1,0:T(8,128)(2,1)S(1)} %get-tuple-element.7.decoded_in), custom_call_target="tpu_custom_call" | custom-call | tf_op jit(solution)/shard_map/pallas_call | solution.py:728

commit v14 on v13

--- a/solution.py
+++ b/solution.py
@@ -547,6 +547,23 @@
     for at, to in enumerate(halo_peers):
         remote(lat, halo.at[at], halo_send, halo_recv, to).start()
     tiles = {(0, 0): lat[...].astype(F32)}
+    seven = kv_stage.at[pl.ds(0, heads - 1)]
+    remote(seven, seven, kv_send, kv_recv, peer).wait_send()
+    seven = q_stage.at[pl.ds(0, heads - 1)]
+    remote(seven, seven, q_a2a_send, q_a2a_recv, peer).wait_send()
+    ring_all = kv.at[pl.ds(0, far - 1)]
+    to_right(ring_all, ring_recv.at[0, 0, 0]).wait_send()
+    to_left(ring_all, ring_recv.at[0, 0, 0]).wait_send()
+    ring_half = kv.at[0, :, 0]
+    to_right(ring_half, ring_recv.at[0, 0, 0], 1).wait_send()
+    to_left(ring_half, ring_recv.at[0, 0, 0], 1).wait_send()
+    seven = qs.at[pl.ds(0, PAIR - 1)]
+    remote(seven, seven, q_send, q_recv, peer).wait_send()
+    await_shares(o_stage, o_send, o_recv, True)
+    await_shares(mark_stage, mark_send, mark_recv, True)
+    for part in range(rs_parts):
+        whole = rs_stage.at[part]
+        remote(whole, whole, rs_send.at[part], rs_recv.at[part], peer).wait_send()
     remote(halo, halo, halo_send, halo_recv, peer).wait_recv()
     for at, (dr, dc) in enumerate(halo_steps):
         tiles[(-dr, -dc)] = halo[at].astype(F32)
@@ -582,23 +599,6 @@
         cols = slice(tile * HEAD_DIM, (tile + 1) * HEAD_DIM)
         decoded[:, :, cols] = pixels[:, tile].astype(BF16)
 
-    seven = kv_stage.at[pl.ds(0, heads - 1)]
-    remote(seven, seven, kv_send, kv_recv, peer).wait_send()
-    seven = q_stage.at[pl.ds(0, heads - 1)]
-    remote(seven, seven, q_a2a_send, q_a2a_recv, peer).wait_send()
-    ring_all = kv.at[pl.ds(0, far - 1)]
-    to_right(ring_all, ring_recv.at[0, 0, 0]).wait_send()
-    to_left(ring_all, ring_recv.at[0, 0, 0]).wait_send()
-    ring_half = kv.at[0, :, 0]
-    to_right(ring_half, ring_recv.at[0, 0, 0], 1).wait_send()
-    to_left(ring_half, ring_recv.at[0, 0, 0], 1).wait_send()
-    seven = qs.at[pl.ds(0, PAIR - 1)]
-    remote(seven, seven, q_send, q_recv, peer).wait_send()
-    await_shares(o_stage, o_send, o_recv, True)
-    await_shares(mark_stage, mark_send, mark_recv, True)
-    for part in range(rs_parts):
-        whole = rs_stage.at[part]
-        remote(whole, whole, rs_send.at[part], rs_recv.at[part], peer).wait_send()
     remote(halo, halo, halo_send, halo_recv, peer).wait_send()
 
 

time: 59.8 us -> 59.8 us (level)
  no operation moved by 1% of the time
where the time goes in v14:
time: 59.8 us; the launch traced here: 59.6 us
  Pallas kernels  59 us (99%)
  between operations  0.64 us (1%)
    pallas_call x1, Pallas kernels, body(): pl.pallas_call(functools.partial(kernel, seqs, heads), out_shape=tuple((p...  58.3 us

profile of v14, /device:TPU:1, one launch (start us, length us, event | category | flops | bytes accessed | tf_op | source)
XLA Modules:
  0.0 59.6 jit_solution(7145721194830506398)
XLA Ops:
  0.6 58.3 %shard_map.167 = (bf16[8,3072]{1,0:T(8,128)(2,1)S(1)}, bf16[2,16,512]{2,1,0:T(8,128)(2,1)S(1)}) custom-call(bf16[8,3072]{1,0:T(8,128)(2,1)} %bitcast.17, bf16[8,3072]{1,0:T(8,128)(2,1)} %bitcast.18, bf16[8,3072]{1,0:T(8,128)(2,1)} %bitcast.19, bf16[256,384]{1,0:T(8,128)(2,1)} %text_k_hbm.1, bf16[256,384]{1,0:T(8,128)(2,1)} %text_v_hbm.1, s32[1,256]{1,0:T(1,128)} %bitcast.28, ...), custom_call_target="tpu_custom_call" | custom-call | flops 1200000000 | bytes 5000000 | tf_op jit(solution)/shard_map/pallas_call | solution.py:671
  59.0 0.7 %shard_map.168 = (bf16[8,3072]{1,0:T(8,128)(2,1)}, bf16[2,16,512]{2,1,0:T(8,128)(2,1)}) custom-call(bf16[8,3072]{1,0:T(8,128)(2,1)S(1)} %get-tuple-element.6.block_in, bf16[2,16,512]{2,1,0:T(8,128)(2,1)S(1)} %get-tuple-element.7.decoded_in), custom_call_target="tpu_custom_call" | custom-call | tf_op jit(solution)/shard_map/pallas_call | solution.py:728

commit v15 on v14

--- a/solution.py
+++ b/solution.py
@@ -280,11 +280,14 @@
     def to_left(ref, recv, send=0):
         return remote(ref, ref, ring_send.at[1] if send == 0 else half_send.at[1], recv, left)
 
-    pieces_of = [(n, part) for n in range(GROUP) for part in range(2)]
+    def piece(slot, n, part):
+        return kv.at[slot, n, part // 2, pl.ds(part % 2 * (rows // 2), rows // 2)]
+
+    pieces_of = [(n, part) for n in range(GROUP) for part in range(4)]
 
     for n, part in pieces_of:
-        to_right(kv.at[z, n, part], ring_recv.at[z, n, part]).start()
-        to_left(kv.at[z, n, part], ring_recv.at[z, n, part]).start()
+        to_right(piece(z, n, part), ring_recv.at[z, n, part]).start()
+        to_left(piece(z, n, part), ring_recv.at[z, n, part]).start()
     for load in loads[7:]:
         load.start()
 
@@ -344,11 +347,11 @@
         other = slot_at(step)
 
         def one_head(n, carry):
-            for part in range(2):
-                copy = to_right(kv.at[one, n, part], ring_recv.at[one, n, part])
+            for part in range(4):
+                copy = to_right(piece(one, n, part), ring_recv.at[one, n, part])
                 copy.wait_recv()
                 copy.start()
-                copy = to_left(kv.at[other, n, part], ring_recv.at[other, n, part])
+                copy = to_left(piece(other, n, part), ring_recv.at[other, n, part])
                 copy.wait_recv()
                 copy.start()
             return carry
@@ -360,14 +363,14 @@
         other = slot_at(step)
 
         def one_head(n, carry):
-            for part in range(2):
-                copy = to_right(kv.at[one, n, part], ring_recv.at[one, n, part], 1)
+            for part in range(4):
+                copy = to_right(piece(one, n, part), ring_recv.at[one, n, part], 1)
                 copy.wait_recv()
-                if part == 0:
+                if part < 2:
                     copy.start()
-                copy = to_left(kv.at[other, n, part], ring_recv.at[other, n, part], 1)
+                copy = to_left(piece(other, n, part), ring_recv.at[other, n, part], 1)
                 copy.wait_recv()
-                if part == 1:
+                if part >= 2:
                     copy.start()
             return carry
 
@@ -413,8 +416,10 @@
     marks[...] = jnp.zeros_like(marks)
 
     def last_step(n, carry):
-        to_right(kv.at[opposite, n, 0], ring_recv.at[opposite, n, 0]).wait_recv()
-        to_left(kv.at[opposite, n, 1], ring_recv.at[opposite, n, 1]).wait_recv()
+        for part in range(2):
+            to_right(piece(opposite, n, part), ring_recv.at[opposite, n, part]).wait_recv()
+        for part in range(2, 4):
+            to_left(piece(opposite, n, part), ring_recv.at[opposite, n, part]).wait_recv()
         top, total, acc = absorb(n, [opposite])
         share = (acc / total).T.astype(BF16)
         for i in range(PAIR):
@@ -706,7 +711,7 @@
             dma,
             dma((2,)),
             dma((2,)),
-            dma((layers, GROUP, 2)),
+            dma((layers, GROUP, 4)),
             dma,
             dma,
             dma,

time: 59.8 us -> 60.4 us (1.010)
    pallas_call x1, Pallas kernels: 58.3 us -> 59 us  [body(): pl.pallas_call(functools.partial(kernel, seqs, heads), out_shape=tuple((p...]
where the time goes in v15:
time: 60.4 us; the launch traced here: 60.3 us
  Pallas kernels  59.6 us (99%)
  between operations  0.64 us (1%)
    pallas_call x1, Pallas kernels, body(): pl.pallas_call(functools.partial(kernel, seqs, heads), out_shape=tuple((p...  59 us

profile of v15, /device:TPU:1, one launch (start us, length us, event | category | flops | bytes accessed | tf_op | source)
XLA Modules:
  0.0 60.3 jit_solution(5750864054949656475)
XLA Ops:
  0.6 59.0 %shard_map.167 = (bf16[8,3072]{1,0:T(8,128)(2,1)S(1)}, bf16[2,16,512]{2,1,0:T(8,128)(2,1)S(1)}) custom-call(bf16[8,3072]{1,0:T(8,128)(2,1)} %bitcast.17, bf16[8,3072]{1,0:T(8,128)(2,1)} %bitcast.18, bf16[8,3072]{1,0:T(8,128)(2,1)} %bitcast.19, bf16[256,384]{1,0:T(8,128)(2,1)} %text_k_hbm.1, bf16[256,384]{1,0:T(8,128)(2,1)} %text_v_hbm.1, s32[1,256]{1,0:T(1,128)} %bitcast.28, ...), custom_call_target="tpu_custom_call" | custom-call | flops 1200000000 | bytes 5000000 | tf_op jit(solution)/shard_map/pallas_call | solution.py:676
  59.6 0.7 %shard_map.168 = (bf16[8,3072]{1,0:T(8,128)(2,1)}, bf16[2,16,512]{2,1,0:T(8,128)(2,1)}) custom-call(bf16[8,3072]{1,0:T(8,128)(2,1)S(1)} %get-tuple-element.6.block_in, bf16[2,16,512]{2,1,0:T(8,128)(2,1)S(1)} %get-tuple-element.7.decoded_in), custom_call_target="tpu_custom_call" | custom-call | tf_op jit(solution)/shard_map/pallas_call | solution.py:733
